TPU v7x, 32 devices: a whole 2x2x4 slice. The times are simulated.
32 devices in a mesh: loop: 16 (over z, y, x), grp: 2 (over core).
Axes of the slice: x: 2, y: 2, z: 4, core: 2. Of those that a mesh axis runs over, the one named last changes fastest.
Arguments:
- particles: bfloat16 [2048, 3456], P('loop'), may hold values from -32 to 32
- references: bfloat16 [64, 3456], P(('loop', 'grp')), may hold values from -6 to 6
- classes: int32 [2048], P(('loop', 'grp')), may hold values from 0 to 63, as said below
- angles: int32 [2048], P(('loop', 'grp')), may hold values from 0 to 71
- weights: int32 [2048], P(('loop', 'grp')), may hold values from 1 to 4
Outputs:
- log_evidence: float32 [2048], P(('loop', 'grp'))
- class_average: float32 [64, 3456], P(('loop', 'grp'))
Inputs may be any that keep to these rules, and one draw needn't show every extreme that they name: Call the classes c with the same value of c // 4 the classes of one owner. In each aligned block of 64 rows at most 8 particles name the classes of one owner, and one owner receives exactly 8 from every block. Every class is named by some particle.
All inputs are finite; a program needn't handle non-finite values.
Results may differ from a plain program's by a relative error of at most 0.0003.
Values may be sent and summed in bfloat16 or wider, within the bound.
A program may use at most 128 MiB of HBM per device.

v0:
```python
import math

import jax
import jax.numpy as jnp
from jax import lax
from jax.sharding import PartitionSpec as P

RADII = 48
ANGLES = 72


score_factor = 2.0


def turned_rows(ref_block, radius_count, angle_count):
    block_rows = ref_block.shape[0]
    polar_rows = ref_block.reshape(block_rows, radius_count, angle_count)
    angle_grid = jnp.arange(angle_count, dtype=jnp.int32)
    source_index = (angle_grid[:, None] + angle_grid[None, :]) % angle_count
    rotated = jnp.take(polar_rows, source_index, axis=2)
    rotated = jnp.transpose(rotated, (0, 2, 1, 3))
    return rotated.reshape(block_rows * angle_count, radius_count * angle_count)


def group_of():
    for group_size in (16, 8, 4, 2):
        return group_size
    return 1


def empty_stats(row_count):
    return (jnp.full((row_count,), -jnp.inf, jnp.float32), jnp.zeros((row_count,), jnp.float32))


def score_all(images, gathered):
    flat_len = images.shape[1]
    score_scale = score_factor / math.sqrt(flat_len)
    ref_count = gathered.shape[0]
    group_size = group_of()
    ref_groups = gathered.reshape(ref_count // group_size, group_size, flat_len)

    def advance(current, ref_block):
        highest, summed = current
        rotated = turned_rows(ref_block, RADII, ANGLES)
        scores = (
            lax.dot_general(
                images, rotated, (((1,), (1,)), ((), ())), preferred_element_type=jnp.float32
            )
            * score_scale
        )
        new_max = jnp.maximum(highest, jnp.max(scores, axis=1))
        summed = summed * jnp.exp(highest - new_max) + jnp.sum(
            jnp.exp(scores - new_max[:, None]), axis=1
        )
        return ((new_max, summed), None)

    result, _ = lax.scan(advance, empty_stats(images.shape[0]), ref_groups)
    return result


def local(particles, references, classes, angles, weights):
    row_count, flat_len = particles.shape
    grp_size = lax.axis_size("grp")
    half_rows = row_count // grp_size
    grp_index = lax.axis_index("grp")
    own_rows = lax.dynamic_slice_in_dim(particles, grp_index * half_rows, half_rows, 0)
    gathered = lax.all_gather(references, "loop", axis=0, tiled=True)
    highest, summed = score_all(particles, gathered)
    joint_max = lax.pmax(highest, "grp")
    summed = lax.psum(summed * jnp.exp(highest - joint_max), "grp")
    highest = joint_max
    highest = lax.dynamic_slice_in_dim(highest, grp_index * half_rows, half_rows, 0)
    summed = lax.dynamic_slice_in_dim(summed, grp_index * half_rows, half_rows, 0)
    log_evidence = highest + jnp.log(summed)
    owner_count = lax.axis_size("loop")
    per_owner = references.shape[0] * grp_size
    capacity = max(2, row_count // owner_count)
    slot_count = owner_count * capacity
    owner_of = classes // per_owner
    member_of = classes % per_owner
    owner_hits = (owner_of[:, None] == jnp.arange(owner_count, dtype=jnp.int32)[None, :]).astype(
        jnp.int32
    )
    earlier = jnp.cumsum(owner_hits, axis=0) - owner_hits
    slot_index = jnp.sum(earlier * owner_hits, axis=1)
    target_slot = owner_of * capacity + slot_index
    placement = (jnp.arange(slot_count, dtype=jnp.int32)[:, None] == target_slot[None, :]).astype(
        jnp.bfloat16
    )
    outgoing = jnp.dot(placement, own_rows, preferred_element_type=jnp.float32).astype(jnp.bfloat16)
    outgoing = outgoing.reshape(owner_count, capacity, flat_len)
    labels = jnp.stack([member_of, angles, weights], axis=1).astype(jnp.bfloat16)
    labels_out = jnp.dot(placement, labels, preferred_element_type=jnp.float32).astype(jnp.bfloat16)
    labels_out = labels_out.reshape(owner_count, capacity, 3)
    incoming, labels_in = (
        lax.all_to_all(outgoing, "loop", split_axis=0, concat_axis=0, tiled=True),
        lax.all_to_all(labels_out, "loop", split_axis=0, concat_axis=0, tiled=True),
    )
    images = incoming.reshape(slot_count, RADII, ANGLES)
    labels_in = labels_in.reshape(slot_count, 3).astype(jnp.float32)
    member_in = labels_in[:, 0]
    rotation = labels_in[:, 1]
    weight_of = labels_in[:, 2]
    angle_grid = jnp.arange(ANGLES, dtype=jnp.float32)
    source_angle = jnp.mod(angle_grid[None, :] - rotation[:, None], float(ANGLES))
    rotator = (angle_grid[None, :, None] == source_angle[:, None, :]).astype(jnp.bfloat16)
    aligned = jnp.einsum("srt,stf->srf", images, rotator, preferred_element_type=jnp.float32)
    aligned = aligned.astype(jnp.bfloat16).reshape(slot_count, flat_len)
    member_grid = jnp.arange(per_owner, dtype=jnp.float32)
    weighted = (
        (member_grid[:, None] == member_in[None, :]).astype(jnp.float32) * weight_of[None, :]
    ).astype(jnp.bfloat16)
    partial_sums = jnp.dot(weighted, aligned, preferred_element_type=jnp.float32)
    partial_weight = jnp.sum(weighted.astype(jnp.float32), axis=1)
    class_sums, class_weight = (
        lax.psum_scatter(partial_sums, "grp", scatter_dimension=0, tiled=True),
        lax.psum_scatter(partial_weight, "grp", scatter_dimension=0, tiled=True),
    )
    class_average = class_sums / class_weight[:, None]
    return (log_evidence, class_average)


def solution(mesh):
    return jax.shard_map(
        local,
        mesh=mesh,
        in_specs=(
            P("loop", None),
            P(("loop", "grp"), None),
            P(("loop", "grp")),
            P(("loop", "grp")),
            P(("loop", "grp")),
        ),
        out_specs=(P(("loop", "grp")), P(("loop", "grp"), None)),
        check_vma=False,
    )
```

profile of v0, /device:TPU:0, one launch (start us, length us, event | category | flops | bytes accessed | tf_op | source)
XLA Modules:
  0.0 239.4 jit_solution(6127622883480263836)
XLA Ops:
  0.6 0.7 fusion.30
  1.3 0.1 fusion.19
  1.4 0.1 reduce_window_sum.11
  1.5 0.2 select_reduce_fusion
  1.7 0.7 convert_bitcast_fusion
  2.3 0.1 convolution_convert_fusion.1
  2.5 0.1 reshape.123
  2.6 0.6 copy.24
  3.2 8.3 %all-to-all-start = ((bf16[16,8,3]{1,2,0:T(4,128)(2,1)}), bf16[16,8,3]{1,2,0:T(4,128)(2,1)S(1)}, u32[]{:S(2)}, u32[]{:S(2)}) async-start(bf16[16,8,3]{1,2,0:T(4,128)(2,1)} %copy.24), calls=%async_computation | async-start | bytes 32768 | tf_op jit(solution)/shard_map/all_to_all | solution.py:97
  11.5 2.3 fusion.10
  13.8 42.4 %all-gather = bf16[16,2,3456]{2,1,0:T(2,128)(2,1)S(1)} all-gather(bf16[1,2,3456]{2,1,0:T(2,128)(2,1)} %bitcast.42), channel_id=1, replica_groups=mesh['loop'=16,'grp'=2] {'loop'}, dimensions={0}, use_global_device_ids=true | all-gather | bytes 235008 | tf_op jit(solution)/shard_map/all_gather | solution.py:67
  56.3 0.1 reshape.122
  56.4 4.3 %all-to-all-start.1 = ((bf16[16,8,3456]{2,1,0:T(8,128)(2,1)}), bf16[16,8,3456]{2,1,0:T(8,128)(2,1)}, u32[]{:S(2)}, u32[]{:S(2)}) async-start(bf16[16,8,3456]{2,1,0:T(8,128)(2,1)} %fusion.10), calls=%async_computation.1 | async-start | bytes 1769472 | tf_op jit(solution)/shard_map/all_to_all | solution.py:96
  60.7 0.0 copy-start.2
  60.7 162.3 %while.15 = (s32[]{:T(128)}, f32[128]{0:T(128)S(1)}, f32[128]{0:T(128)S(1)}, bf16[2,16,3456]{2,1,0:T(8,128)(2,1)S(1)}, bf16[128,3456]{1,0:T(8,128)(2,1)}, /*index=5*/s32[]{:T(128)}, s32[]{:T(128)}) while((s32[]{:T(128)}, f32[128]{0:T(128)S(1)}, f32[128]{0:T(128)S(1)}, bf16[2,16,3456]{2,1,0:T(8,128)(2,1)S(1)}, ...), condition=%wide.region_3.4_spmd.clone, body=%wide.region_0.3_spmd.clone.sunk | while | flops 1023913024 | bytes 78075904 | solution.py:57
  60.8 0.3 reshape.155
  61.1 0.3 copy.30
  61.4 0.1 reshape.156
  61.5 16.7 %gather_fusion = bf16[5184,16,48]{2,1,0:T(8,128)(2,1)} fusion(bf16[16,48,72]{1,0,2:T(8,128)(2,1)S(1)} %copy.30, s32[6144]{0:T(1024)S(1)} %pad_clamp_fusion.2), kind=kCustom, calls=%fused_computation.clone.clone.1 | custom fusion | bytes 15945984 | tf_op jit(solution)/shard_map/while/body/eval_jaxpr/jit(_take)/gather | solution.py:20
  78.3 24.6 %copy.31 = bf16[72,72,16,48]{1,3,0,2:T(8,128)(2,1)} copy(bf16[72,72,16,48]{3,2,1,0:T(8,128)(2,1)} %bitcast.40) | data formatting | bytes 15925248 | tf_op jit(solution)/shard_map/while/body/eval_jaxpr/jit(_take)/gather | solution.py:20
  103.0 10.6 %select_bitcast_fusion.2 = bf16[16,72,48,72]{3,2,1,0:T(8,128)(2,1)} fusion(bf16[72,72,16,48]{1,3,0,2:T(8,128)(2,1)} %copy.31, pred[72,72]{1,0:T(8,128)(4,1)S(1)} %compare_and_fusion.2), kind=kLoop, calls=%fused_computation.1.clone.1 | loop fusion | flops 3981312 | bytes 15930432 | tf_op jit(solution)/shard_map/while/body/eval_jaxpr/jit(_take)/select_n | solution.py:20
  113.6 22.6 %reshape.157 = bf16[1152,3456]{1,0:T(8,128)(2,1)} reshape(bf16[16,72,48,72]{3,2,1,0:T(8,128)(2,1)} %select_bitcast_fusion.2) | data formatting | bytes 15925248 | tf_op jit(solution)/shard_map/while/body/eval_jaxpr/reshape | solution.py:22
  136.2 5.5 %fusion.46 = (f32[128]{0:T(128)S(1)}, f32[1152,128]{1,0:T(8,128)S(1)}) fusion(bf16[1152,3456]{1,0:T(8,128)(2,1)} %reshape.157, bf16[128,3456]{1,0:T(8,128)(2,1)S(1)} %copy-done), kind=kOutput, calls=%fused_computation.74.clone.1 | convolution fusion | flops 1019510656 | bytes 9437696 | tf_op jit(solution)/shard_map/while/body/eval_jaxpr/dot_general | solution.py:46
  141.7 0.2 exponential_reduce_fusion.2
  141.9 0.3 reshape.155
  142.3 0.3 copy.30
  142.6 0.1 reshape.156
  142.7 16.7 %gather_fusion = bf16[5184,16,48]{2,1,0:T(8,128)(2,1)} fusion(bf16[16,48,72]{1,0,2:T(8,128)(2,1)S(1)} %copy.30, s32[6144]{0:T(1024)S(1)} %pad_clamp_fusion.2), kind=kCustom, calls=%fused_computation.clone.clone.1 | custom fusion | bytes 15945984 | tf_op jit(solution)/shard_map/while/body/eval_jaxpr/jit(_take)/gather | solution.py:20
  159.5 24.6 %copy.31 = bf16[72,72,16,48]{1,3,0,2:T(8,128)(2,1)} copy(bf16[72,72,16,48]{3,2,1,0:T(8,128)(2,1)} %bitcast.40) | data formatting | bytes 15925248 | tf_op jit(solution)/shard_map/while/body/eval_jaxpr/jit(_take)/gather | solution.py:20
  184.1 10.6 %select_bitcast_fusion.2 = bf16[16,72,48,72]{3,2,1,0:T(8,128)(2,1)} fusion(bf16[72,72,16,48]{1,3,0,2:T(8,128)(2,1)} %copy.31, pred[72,72]{1,0:T(8,128)(4,1)S(1)} %compare_and_fusion.2), kind=kLoop, calls=%fused_computation.1.clone.1 | loop fusion | flops 3981312 | bytes 15930432 | tf_op jit(solution)/shard_map/while/body/eval_jaxpr/jit(_take)/select_n | solution.py:20
  194.8 22.6 %reshape.157 = bf16[1152,3456]{1,0:T(8,128)(2,1)} reshape(bf16[16,72,48,72]{3,2,1,0:T(8,128)(2,1)} %select_bitcast_fusion.2) | data formatting | bytes 15925248 | tf_op jit(solution)/shard_map/while/body/eval_jaxpr/reshape | solution.py:22
  217.3 5.5 %fusion.46 = (f32[128]{0:T(128)S(1)}, f32[1152,128]{1,0:T(8,128)S(1)}) fusion(bf16[1152,3456]{1,0:T(8,128)(2,1)} %reshape.157, bf16[128,3456]{1,0:T(8,128)(2,1)S(1)} %copy-done), kind=kOutput, calls=%fused_computation.74.clone.1 | convolution fusion | flops 1019510656 | bytes 9437696 | tf_op jit(solution)/shard_map/while/body/eval_jaxpr/dot_general | solution.py:46
  222.9 0.2 exponential_reduce_fusion.2
  223.1 0.6 dynamic-slice
  224.3 2.5 %pmax.7 = f32[128]{0:T(128)S(1)} all-reduce(f32[128]{0:T(128)S(1)} %get-tuple-element.69), channel_id=1, replica_groups=mesh['loop'=16,'grp'=2] {'grp'}, use_global_device_ids=true, to_apply=%region_4.5 | all-reduce | flops 128 | bytes 1024 | tf_op jit(solution)/shard_map/pmax | solution.py:69
  226.8 0.8 copy.25
  227.6 0.1 copy.26
  227.7 0.1 reshape.127
  227.8 0.1 convert_reduce_fusion
  227.9 0.1 add_select_fusion.2
  228.0 4.0 %reshape.125 = bf16[128,48,72]{2,1,0:T(8,128)(2,1)S(1)} reshape(bf16[16,8,3456]{2,1,0:T(8,128)(2,1)} %all-to-all-done.1) | data formatting | bytes 1769472 | tf_op jit(solution)/shard_map/reshape | solution.py:99
  232.0 1.0 fusion.12
  233.0 1.0 copy.27
  234.1 0.3 fusion.20
  234.4 3.6 %all-reduce.2 = (f32[128]{0:T(128)S(1)}, f32[4,3456]{1,0:T(4,128)S(1)}, f32[4]{0:T(128)S(1)}) all-reduce(f32[128]{0:T(128)S(1)} %exponential_multiply_fusion, f32[4,3456]{1,0:T(4,128)S(1)} %fusion.20, f32[4]{0:T(128)S(1)} %convert_reduce_fusion), channel_id=1, replica_groups=mesh['loop'=16,'grp'=2] {'grp'}, use_global_device_ids=true, to_apply=%region_5.6 | all-reduce | flops 13956 | bytes 111648 | tf_op jit(solution)/shard_map/psum | solution.py:70
  238.0 0.6 log_add_fusion
  238.6 0.1 dynamic-slice.3
  238.7 0.7 dynamic-slice_divide_fusion
  (29 shorter events, 0.3 us)
Async XLA Ops:
  3.2 53.2 %all-to-all-start = ((bf16[16,8,3]{1,2,0:T(4,128)(2,1)}), bf16[16,8,3]{1,2,0:T(4,128)(2,1)S(1)}, u32[]{:S(2)}, u32[]{:S(2)}) async-start(bf16[16,8,3]{1,2,0:T(4,128)(2,1)} %copy.24), calls=%async_computation | async-start | bytes 32768 | tf_op jit(solution)/shard_map/all_to_all | solution.py:97
  56.4 4.3 %copy-start.1 = (bf16[16,8,3]{1,2,0:T(4,128)(2,1)}, bf16[16,8,3]{1,2,0:T(4,128)(2,1)S(1)}, u32[]{:S(2)}) copy-start(bf16[16,8,3]{1,2,0:T(4,128)(2,1)S(1)} %all-to-all-done) | copy-start | bytes 2308
  56.4 171.6 %all-to-all-start.1 = ((bf16[16,8,3456]{2,1,0:T(8,128)(2,1)}), bf16[16,8,3456]{2,1,0:T(8,128)(2,1)}, u32[]{:S(2)}, u32[]{:S(2)}) async-start(bf16[16,8,3456]{2,1,0:T(8,128)(2,1)} %fusion.10), calls=%async_computation.1 | async-start | bytes 1769472 | tf_op jit(solution)/shard_map/all_to_all | solution.py:96
  60.7 162.4 %copy-start.2 = (u32[32]{0:T(128)S(1)}, u32[32]{0:T(128)}, u32[]{:S(2)}) copy-start(u32[32]{0:T(128)} %constant.127) | copy-start | bytes 388
  113.6 22.6 %copy-start = (bf16[128,3456]{1,0:T(8,128)(2,1)S(1)}, bf16[128,3456]{1,0:T(8,128)(2,1)}, u32[]{:S(2)}) copy-start(bf16[128,3456]{1,0:T(8,128)(2,1)} %get-tuple-element.163) | copy-start | bytes 2654212 | tf_op jit(solution)/shard_map/while
  194.8 22.6 %copy-start = (bf16[128,3456]{1,0:T(8,128)(2,1)S(1)}, bf16[128,3456]{1,0:T(8,128)(2,1)}, u32[]{:S(2)}) copy-start(bf16[128,3456]{1,0:T(8,128)(2,1)} %get-tuple-element.163) | copy-start | bytes 2654212 | tf_op jit(solution)/shard_map/while
where the time goes:
time: 242 us; the launch traced here: 239 us
  local copies, waits for them, and re-layouts  137 us (57%)
  blocking collectives  48.5 us (20%)
  other arithmetic  25 us (10%)
  matrix products  14.8 us (6%)
  starting transfers between devices  12.6 us (5%)
    gather x4, local copies, waits for them, and re-layouts, turned_rows(): rotated = jnp.take(polar_rows, source_index, axis=2)  82.7 us
    reshape x2, local copies, waits for them, and re-layouts, turned_rows(): return rotated.reshape(block_rows * angle_count, radius_count * angle_count)  45.1 us
    all_gather x1, blocking collectives, local(): gathered = lax.all_gather(references, 'loop', axis=0, tiled=True)  42.4 us
    select_n x4, other arithmetic, turned_rows(): rotated = jnp.take(polar_rows, source_index, axis=2)  21.3 us
    dot_general x2, matrix products, advance(): lax.dot_general(images, rotated, (((1,), (1,)), ((), ())), preferred_elem...  11 us
    all_to_all x1, starting transfers between devices, local(): lax.all_to_all(labels_out, 'loop', split_axis=0, concat_axis=0, tiled=True)  8.31 us
  transfers between devices with their start and end apart: 2, of which 0 were waited for; matrix products, arithmetic and copies ran while one was open for 69% of the time, Pallas kernels for 0%

commit v1 on v0

v1 whole, which is shorter than its diff:
```python
import functools
import math

import jax
import jax.numpy as jnp
from jax import lax
from jax.experimental import pallas as pl
from jax.experimental.pallas import tpu as pltpu
from jax.sharding import PartitionSpec as P

RADII = 48
ANGLES = 72
FLAT = RADII * ANGLES
LANES = 128
TILES = FLAT // LANES
WIRE = 32
STEP = 8
TURNS = ANGLES // STEP
EXT = STEP - 2
SCALE = 2.0 / math.sqrt(FLAT)
MESH = pl.DeviceIdType.MESH


def kernel(
    n, cls_dev,
    x_ref, ref_ref, cls_ref, ang_ref, wgt_ref,
    logev_ref, avg_ref,
    wire, wide, rbig, lab, stat, flat_t, ping, pong, alig, ptx, part, got,
    r_send, r_recv, s_send, s_recv, c_send, c_recv,
):
    me = lax.axis_index("loop")
    grp = lax.axis_index("grp")
    other = 1 - grp
    rows = x_ref.shape[0]
    half = rows // 2
    cls_count = n * cls_dev

    def peer(k):
        return {"loop": lax.rem(me + k, n)}

    def ref_copy(k):
        return pltpu.make_async_remote_copy(
            src_ref=wire.at[0], dst_ref=wire.at[k], send_sem=r_send.at[k], recv_sem=r_recv.at[k],
            device_id=peer(k), device_id_type=MESH)

    def sum_copy(k):
        return pltpu.make_async_remote_copy(
            src_ref=part.at[lax.rem(me + k, n)], dst_ref=got.at[k], send_sem=s_send.at[k],
            recv_sem=s_recv.at[k], device_id=peer(k), device_id_type=MESH)

    def core_copy(buf, k):
        return pltpu.make_async_remote_copy(
            src_ref=buf.at[0], dst_ref=buf.at[1], send_sem=c_send.at[k], recv_sem=c_recv.at[k],
            device_id={"grp": other}, device_id_type=MESH)

    barrier = pltpu.get_barrier_semaphore()

    @pl.loop(1, n)
    def _(k):
        pl.semaphore_signal(barrier, inc=1, device_id=peer(k), device_id_type=MESH)

    pl.semaphore_signal(barrier, inc=1, device_id={"grp": other}, device_id_type=MESH)

    wire[0] = ref_ref[...]
    lane = lax.broadcasted_iota(jnp.int32, (1, rows), 1)
    mine = (lane // half) == grp
    for i, src in enumerate((cls_ref, ang_ref, wgt_ref)):
        both = jnp.concatenate([src[...], src[...]], axis=1)
        lab[0, i:i + 1, :] = jnp.where(mine, both, 0)

    pl.semaphore_wait(barrier, n)

    label_copy = core_copy(lab, 0)
    label_copy.start()

    @pl.loop(1, n)
    def _(k):
        ref_copy(k).start()

    for i in range(TILES):
        tile = x_ref[:, i * LANES:(i + 1) * LANES].astype(jnp.float32)
        flat_t[i * LANES:(i + 1) * LANES, :] = tile.T

    for t in range(ANGLES):
        rad = flat_t[pl.ds(t, RADII, stride=ANGLES), :]
        ping[t] = rad
        low = rad.astype(jnp.bfloat16)
        for shift in range(2):
            for at in (t + shift + EXT, t + shift + EXT - ANGLES):
                if 0 <= at < ANGLES + EXT:
                    ptx[at * RADII:(at + 1) * RADII, shift * rows:(shift + 1) * rows] = low

    label_copy.wait()
    labels = lab[0, 0:8, :] + lab[1, 0:8, :]
    classes, angles, weights = labels[0:1], labels[1:2], labels[2:3]

    src, dst = ping, pong
    for bit in range(7):
        on = jnp.broadcast_to(((angles >> bit) & 1) == 1, (8, rows))
        by = 1 << bit

        def turn(t, _, src=src, dst=dst, on=on, by=by):
            back = lax.rem(t + (ANGLES - by), ANGLES)
            for j in range(RADII // 8):
                rs = slice(j * 8, (j + 1) * 8)
                dst[t, rs, :] = jnp.where(on, src[back, rs, :], src[t, rs, :])
            return 0

        lax.fori_loop(0, ANGLES, turn, 0, unroll=4)
        src, dst = dst, src

    for t in range(ANGLES):
        flat_t[pl.ds(t, RADII, stride=ANGLES), :] = src[t]
    alig[0:FLAT, :] = flat_t[...].astype(jnp.bfloat16)
    alig[FLAT:, :] = jnp.ones((LANES, rows), jnp.bfloat16)

    row = lax.broadcasted_iota(jnp.int32, (cls_count, rows), 0)
    named = (row // cls_dev) * (2 * cls_dev) + grp * cls_dev + row % cls_dev
    pick = jnp.where(named == classes, weights, 0).astype(jnp.float32).astype(jnp.bfloat16)
    chunk = 512
    for i in range((FLAT + LANES) // chunk):
        sl = slice(i * chunk, (i + 1) * chunk)
        sums = lax.dot_general(pick, alig[sl, :], (((1,), (1,)), ((), ())),
                               preferred_element_type=jnp.float32)
        for o in range(n):
            part[o, :, sl] = sums[o * cls_dev:(o + 1) * cls_dev, :]

    @pl.loop(1, n)
    def _(k):
        sum_copy(k).start()

    @pl.loop(1, n)
    def _(k):
        ref_copy(k).wait()

    wide[...] = wire[...].reshape(n * cls_dev * WIRE, LANES).astype(jnp.float32)
    for i in range(TILES):
        tile = wide[pl.ds(i, cls_count, stride=WIRE), :].astype(jnp.bfloat16)
        for s1 in range(TURNS):
            at = (i - 3 * s1) % TILES
            rbig[s1 * cls_count:(s1 + 1) * cls_count, at * LANES:(at + 1) * LANES] = tile

    tops, mass = [], []
    for q in range(STEP // 2):
        at = (EXT - 2 * q) * RADII
        score = jnp.dot(rbig[...], ptx[at:at + FLAT, :], preferred_element_type=jnp.float32) * SCALE
        top = jnp.max(score, axis=0, keepdims=True)
        total = jnp.sum(jnp.exp(score - top), axis=0, keepdims=True)
        for h in range(2):
            tops.append(top[:, h * rows:(h + 1) * rows])
            mass.append(total[:, h * rows:(h + 1) * rows])
    top = functools.reduce(jnp.maximum, tops)
    total = functools.reduce(jnp.add, [m * jnp.exp(t - top) for t, m in zip(tops, mass)])
    stat[0, 0:1, :] = top
    stat[0, 1:2, :] = total
    stat_copy = core_copy(stat, 1)
    stat_copy.start()

    @pl.loop(1, n)
    def _(k):
        sum_copy(k).wait()

    acc = part[me]
    for k in range(1, n):
        acc = acc + got[k]
    avg_ref[...] = acc[:, :FLAT] / acc[:, FLAT:FLAT + 1]

    stat_copy.wait()
    top2, total2 = stat[1, 0:1, :], stat[1, 1:2, :]
    high = jnp.maximum(top, top2)
    out = high + jnp.log(total * jnp.exp(top - high) + total2 * jnp.exp(top2 - high))
    logev_ref[...] = jnp.where(grp == 0, out[:, :half], out[:, half:])


def local(particles, references, classes, angles, weights):
    rows = particles.shape[0]
    half = rows // 2
    cls_dev = references.shape[0]
    n = lax.axis_size("loop")
    cls_count = n * cls_dev
    polar = references.reshape(cls_dev, RADII, ANGLES).transpose(0, 2, 1).reshape(cls_dev, TILES, LANES)
    polar = jnp.pad(polar, ((0, 0), (0, WIRE - TILES), (0, 0))).reshape(cls_dev * WIRE, LANES)
    vmem = pl.BlockSpec(memory_space=pltpu.VMEM)
    f32, bf16 = jnp.float32, jnp.bfloat16
    logev, avg = pl.pallas_call(
        functools.partial(kernel, n, cls_dev),
        out_shape=(
            jax.ShapeDtypeStruct((1, half), f32),
            jax.ShapeDtypeStruct((cls_dev, FLAT), f32),
        ),
        in_specs=[vmem] * 5,
        out_specs=(vmem, vmem),
        scratch_shapes=[
            pltpu.VMEM((n, cls_dev * WIRE, LANES), bf16),
            pltpu.VMEM((n * cls_dev * WIRE, LANES), f32),
            pltpu.VMEM((TURNS * cls_count, FLAT), bf16),
            pltpu.VMEM((2, 8, rows), jnp.int32),
            pltpu.VMEM((2, 8, rows), f32),
            pltpu.VMEM((FLAT, rows), f32),
            pltpu.VMEM((ANGLES, RADII, rows), f32),
            pltpu.VMEM((ANGLES, RADII, rows), f32),
            pltpu.VMEM((FLAT + LANES, rows), bf16),
            pltpu.VMEM(((ANGLES + EXT) * RADII, 2 * rows), bf16),
            pltpu.VMEM((n, cls_dev, FLAT + LANES), f32),
            pltpu.VMEM((n, cls_dev, FLAT + LANES), f32),
            pltpu.SemaphoreType.DMA((n,)),
            pltpu.SemaphoreType.DMA((n,)),
            pltpu.SemaphoreType.DMA((n,)),
            pltpu.SemaphoreType.DMA((n,)),
            pltpu.SemaphoreType.DMA((2,)),
            pltpu.SemaphoreType.DMA((2,)),
        ],
        compiler_params=pltpu.CompilerParams(
            collective_id=0, has_side_effects=True, vmem_limit_bytes=56 * 1024 * 1024),
    )(particles, polar, classes.reshape(1, half), angles.reshape(1, half), weights.reshape(1, half))
    return logev.reshape(half), avg


def solution(mesh):
    return jax.shard_map(
        local,
        mesh=mesh,
        in_specs=(
            P("loop", None),
            P(("loop", "grp"), None),
            P(("loop", "grp")),
            P(("loop", "grp")),
            P(("loop", "grp")),
        ),
        out_specs=(P(("loop", "grp")), P(("loop", "grp"), None)),
        check_vma=False,
    )
```

time: 242 us -> 28.6 us (0.12)
  the two profiles are of different devices: /device:TPU:0 before, /device:TPU:15 now
where the time goes in v1:
time: 28.6 us; the launch traced here: 28.3 us
  Pallas kernels  23.5 us (82%)
  local copies, waits for them, and re-layouts  4.14 us (14%)
  between operations  0.66 us (2%)
    pallas_call x1, Pallas kernels, local(): pl.pallas_call(functools.partial(kernel, n, cls_dev), out_shape=(jax.Shap...  23.5 us
    unnamed x4, local copies, waits for them, and re-layouts  2.49 us
    reshape x3, local copies, waits for them, and re-layouts, local(): references.reshape(cls_dev, RADII, ANGLES).transpose(0, 2, 1)  1.03 us
    pad x1, local copies, waits for them, and re-layouts, local(): jnp.pad(polar, ((0, 0), (0, WIRE - TILES), (0, 0)))  0.62 us

profile of v1, /device:TPU:15, one launch (start us, length us, event | category | flops | bytes accessed | tf_op | source)
XLA Modules:
  0.0 28.3 jit_solution(17012232284885178872)
XLA Ops:
  0.6 0.8 %reshape.25 = bf16[2,48,72]{2,1,0:T(8,128)(2,1)S(1)} reshape(bf16[2,3456]{1,0:T(2,128)(2,1)} %param.6) | data formatting | bytes 27648 | tf_op jit(solution)/shard_map/reshape | solution.py:181
  1.5 0.1 copy.8
  1.6 0.1 reshape.26
  1.7 0.6 %pad.4 = bf16[2,32,128]{2,1,0:T(8,128)(2,1)} pad(bf16[2,27,128]{2,1,0:T(8,128)(2,1)S(1)} %reshape.26, bf16[]{:T(256)} %constant.2.clone.1), padding=0_0x0_5x0_0 | pad | bytes 30210 | tf_op jit(solution)/shard_map/jit(_pad)/pad | solution.py:182
  2.3 23.5 %shard_map.68 = (f32[1,64]{1,0:T(1,128)}, f32[2,3456]{1,0:T(2,128)}) custom-call(bf16[128,3456]{1,0:T(8,128)(2,1)} %x_ref.1, bf16[64,128]{1,0:T(8,128)(2,1)} %bitcast.7, s32[1,64]{1,0:T(1,128)} %bitcast.8, s32[1,64]{1,0:T(1,128)} %bitcast.9, s32[1,64]{1,0:T(1,128)} %bitcast.10), custom_call_target="tpu_custom_call" | custom-call | tf_op jit(solution)/shard_map/pallas_call | solution.py:185
  25.8 0.0 copy-start
  25.8 0.6 %copy-done = f32[1,64]{1,0:T(1,128)S(1)} copy-done((f32[1,64]{1,0:T(1,128)S(1)}, f32[1,64]{1,0:T(1,128)}, u32[]{:S(2)}) %copy-start) | copy-done | bytes 280
  26.5 0.5 %copy.11 = f32[64]{0:T(128)} copy(f32[64]{0:T(128)S(1)} %bitcast.11) | data formatting | bytes 512
  27.0 1.4 %copy.12 = f32[2,3456]{1,0:T(2,128)} copy(f32[2,3456]{1,0:T(2,128)} %get-tuple-element.9) | data formatting | bytes 55296
Async XLA Ops:
  25.8 0.6 %copy-start = (f32[1,64]{1,0:T(1,128)S(1)}, f32[1,64]{1,0:T(1,128)}, u32[]{:S(2)}) copy-start(f32[1,64]{1,0:T(1,128)} %get-tuple-element.4) | copy-start | bytes 772

commit v2 on v1

v2 whole, which is shorter than its diff:
```python
import functools
import math

import jax
import jax.numpy as jnp
from jax import lax
from jax.experimental import pallas as pl
from jax.experimental.pallas import tpu as pltpu
from jax.sharding import PartitionSpec as P

RADII = 48
ANGLES = 72
FLAT = RADII * ANGLES
LANES = 128
TILES = FLAT // LANES
WIRE = 32
STEP = 8
TURNS = ANGLES // STEP
EXT = STEP - 2
CHUNKS = 3
CHUNK_R = RADII // CHUNKS
CHUNK = FLAT // CHUNKS
WINDOW = 24
INNER = 4
SCALE = 2.0 / math.sqrt(FLAT)
MESH = pl.DeviceIdType.MESH


def chunk_lanes(g):
    return CHUNK + (LANES if g == 0 else 0)


def kernel(
    ni, no, cls_dev,
    x_ref, ref_ref, cls_ref, ang_ref, wgt_ref,
    out_ref,
    square, turned, wide, wire, rbig, lab, stat, flat_t, ping, flat_a, ptx,
    part0, part1, part2, gota0, gota1, gota2, sum0, sum1, sum2, gotb0, gotb1, gotb2,
    z_send, z_recv, i_send, i_recv, f_send, f_recv, a_send, a_recv, b_send, b_recv, c_send, c_recv,
):
    part, gota = (part0, part1, part2), (gota0, gota1, gota2)
    sums, gotb = (sum0, sum1, sum2), (gotb0, gotb1, gotb2)
    me = lax.axis_index("loop")
    grp = lax.axis_index("grp")
    outer, inner = me // ni, lax.rem(me, ni)
    rows = x_ref.shape[0]
    half = rows // 2
    cls_count = ni * no * cls_dev

    def outer_peer(k):
        return {"loop": lax.rem(outer + k, no) * ni + inner}

    def inner_peer(k):
        return {"loop": outer * ni + lax.rem(inner + k, ni)}

    other = {"grp": 1 - grp}

    def remote(src, dst, send, recv, to):
        return pltpu.make_async_remote_copy(
            src_ref=src, dst_ref=dst, send_sem=send, recv_sem=recv, device_id=to, device_id_type=MESH)

    def z_copy(k):
        return remote(wire.at[0, 0], wire.at[0, k], z_send.at[k], z_recv.at[k], outer_peer(k))

    def i_copy(k):
        return remote(wire.at[0, 0], wire.at[k, 0], i_send.at[k], i_recv.at[k], inner_peer(k))

    def f_copy(k):
        return remote(wire.at[0, 1:], wire.at[k, 1:], f_send.at[k], f_recv.at[k], inner_peer(k))

    def a_copy(g, k):
        return remote(part[g].at[lax.rem(inner + k, ni)], gota[g].at[k],
                      a_send.at[g, k], a_recv.at[g, k], inner_peer(k))

    def b_copy(g, k):
        return remote(sums[g].at[lax.rem(outer + k, no)], gotb[g].at[k],
                      b_send.at[g, k], b_recv.at[g, k], outer_peer(k))

    def core_copy(buf, k):
        return remote(buf.at[0], buf.at[1], c_send.at[k], c_recv.at[k], other)

    barrier = pltpu.get_barrier_semaphore()

    @pl.loop(1, no)
    def _(k):
        pl.semaphore_signal(barrier, inc=1, device_id=outer_peer(k), device_id_type=MESH)

    for k in range(1, ni):
        pl.semaphore_signal(barrier, inc=1, device_id=inner_peer(k), device_id_type=MESH)
    pl.semaphore_signal(barrier, inc=1, device_id=other, device_id_type=MESH)

    lane = lax.broadcasted_iota(jnp.int32, (1, rows), 1)
    mine = (lane // half) == grp
    lab[0] = jnp.zeros((8, rows), jnp.int32)
    for i, src in enumerate((cls_ref, ang_ref, wgt_ref)):
        both = jnp.concatenate([src[...], src[...]], axis=1)
        lab[0, i:i + 1, :] = jnp.where(mine, both, 0)

    refs = ref_ref[...].astype(jnp.float32)
    square[...] = jnp.zeros((LANES, LANES), jnp.float32)
    wide[0:cls_dev * WIRE, :] = jnp.zeros((cls_dev * WIRE, LANES), jnp.float32)
    for c in range(cls_dev):
        for r in range(RADII):
            square[r:r + 1, 0:ANGLES] = refs[c:c + 1, r * ANGLES:(r + 1) * ANGLES]
        turned[...] = square[...].T
        line = jnp.concatenate(
            [turned[pl.ds(v, TURNS, stride=STEP), :][:, 0:RADII] for v in range(STEP)], axis=1)
        for w in range(3):
            wide[pl.ds(c * WIRE + w, TURNS, stride=3), :] = line[:, w * LANES:(w + 1) * LANES]
    wire[0, 0] = wide[0:cls_dev * WIRE, :].astype(jnp.bfloat16)

    def transpose(g):
        for i in range(g * (CHUNK // LANES), (g + 1) * (CHUNK // LANES)):
            tile = x_ref[:, i * LANES:(i + 1) * LANES].astype(jnp.float32)
            flat_t[i * LANES:(i + 1) * LANES, :] = tile.T

    transpose(0)
    pl.semaphore_wait(barrier, ni + no - 1)

    label_copy = core_copy(lab, 0)
    label_copy.start()

    @pl.loop(1, no)
    def _(k):
        z_copy(k).start()

    for k in range(1, ni):
        i_copy(k).start()

    transpose(1)
    transpose(2)

    label_copy.wait()
    labels = lab[0] + lab[1]
    classes, angles, weights = labels[0:1], labels[1:2], labels[2:3]
    bits = [jnp.broadcast_to(((angles >> b) & 1) == 1, (8, rows)) for b in range(7)]

    row = lax.broadcasted_iota(jnp.int32, (cls_count, rows), 0)
    owner = row // cls_dev
    named = (((owner % no) * ni + owner // no) * 2 + grp) * cls_dev + row % cls_dev
    pick = jnp.where(named == classes, weights, 0).astype(jnp.float32).astype(jnp.bfloat16)

    def chunk_sums(g):
        for r in range(g * CHUNK_R, (g + 1) * CHUNK_R, 8):
            base = r * ANGLES
            for t0 in range(0, ANGLES, WINDOW):
                vals = {t: flat_t[pl.ds(base + t % ANGLES, 8, stride=ANGLES), :]
                        for t in range(t0 - 7, t0 + WINDOW)}
                for b in range(3):
                    low = t0 - 7 + (2 << b) - 1
                    vals = {t: jnp.where(bits[b], vals[t - (1 << b)], vals[t])
                            for t in range(low, t0 + WINDOW)}
                for t in range(t0, t0 + WINDOW):
                    ping[t] = vals[t]
            for v in range(STEP):
                vals = [ping[STEP * u + v] for u in range(TURNS)]
                for b in range(4):
                    vals = [jnp.where(bits[3 + b], vals[(u - (1 << b)) % TURNS], vals[u])
                            for u in range(TURNS)]
                for u in range(TURNS):
                    flat_a[pl.ds(base + STEP * u + v, 8, stride=ANGLES), :] = vals[u]
        aligned = flat_a[g * CHUNK:(g + 1) * CHUNK, :].astype(jnp.bfloat16)
        if g == 0:
            aligned = jnp.concatenate([aligned, jnp.ones((LANES, rows), jnp.bfloat16)], axis=0)
        mine_sums = lax.dot_general(pick, aligned, (((1,), (1,)), ((), ())),
                                    preferred_element_type=jnp.float32)
        for o in range(ni * no):
            part[g][o // no, o % no] = mine_sums[o * cls_dev:(o + 1) * cls_dev, :]
        for k in range(1, ni):
            a_copy(g, k).start()

    chunk_sums(0)

    @pl.loop(1, no)
    def _(k):
        z_copy(k).wait()

    for k in range(1, ni):
        f_copy(k).start()

    for g in range(1, CHUNKS):
        chunk_sums(g)

    for t in range(ANGLES):
        low = flat_t[pl.ds(t, RADII, stride=ANGLES), :].astype(jnp.bfloat16)
        for shift in range(2):
            for at in (t + shift + EXT, t + shift + EXT - ANGLES):
                if 0 <= at < ANGLES + EXT:
                    ptx[at * RADII:(at + 1) * RADII, shift * rows:(shift + 1) * rows] = low

    def second(g):
        for k in range(1, ni):
            a_copy(g, k).wait()
        acc = part[g][inner]
        for k in range(1, ni):
            acc = acc + gota[g][k]
        sums[g][...] = acc

        @pl.loop(1, no)
        def _(k):
            b_copy(g, k).start()

    second(0)

    for k in range(1, ni):
        i_copy(k).wait()
        f_copy(k).wait()

    wide[...] = wire[...].reshape(cls_count * WIRE, LANES).astype(jnp.float32)
    for i in range(TILES):
        tile = wide[pl.ds(i, cls_count, stride=WIRE), :].astype(jnp.bfloat16)
        for s1 in range(TURNS):
            at = (i - 3 * s1) % TILES
            rbig[s1 * cls_count:(s1 + 1) * cls_count, at * LANES:(at + 1) * LANES] = tile

    tops, mass = [], []
    for q in range(STEP // 2):
        at = (EXT - 2 * q) * RADII
        score = jnp.dot(rbig[...], ptx[at:at + FLAT, :], preferred_element_type=jnp.float32) * SCALE
        top = jnp.max(score, axis=0, keepdims=True)
        total = jnp.sum(jnp.exp(score - top), axis=0, keepdims=True)
        for h in range(2):
            tops.append(top[:, h * rows:(h + 1) * rows])
            mass.append(total[:, h * rows:(h + 1) * rows])
        if q + 1 < CHUNKS:
            second(q + 1)
    top = functools.reduce(jnp.maximum, tops)
    total = functools.reduce(jnp.add, [m * jnp.exp(t - top) for t, m in zip(tops, mass)])
    stat[0] = jnp.concatenate([top, total, jnp.zeros((6, rows), jnp.float32)], axis=0)
    stat_copy = core_copy(stat, 1)
    stat_copy.start()

    weight = None
    for g in range(CHUNKS):
        @pl.loop(1, no)
        def _(k):
            b_copy(g, k).wait()

        acc = sums[g][outer]
        for k in range(1, no):
            acc = acc + gotb[g][k]
        if weight is None:
            weight = acc[:, CHUNK:CHUNK + 1]
        out_ref[:, g * CHUNK:(g + 1) * CHUNK] = acc[:, :CHUNK] / weight

    stat_copy.wait()
    top2, total2 = stat[1, 0:1, :], stat[1, 1:2, :]
    high = jnp.maximum(top, top2)
    out = high + jnp.log(total * jnp.exp(top - high) + total2 * jnp.exp(top2 - high))
    out = jnp.where(grp == 0, out, jnp.concatenate([out[:, half:], out[:, :half]], axis=1))
    out_ref[:, FLAT:] = jnp.broadcast_to(out, (cls_dev, rows))


def local(particles, references, classes, angles, weights):
    rows = particles.shape[0]
    half = rows // 2
    cls_dev = references.shape[0]
    n = lax.axis_size("loop")
    ni = INNER
    no = n // ni
    cls_count = n * cls_dev
    vmem = pl.BlockSpec(memory_space=pltpu.VMEM)
    f32, bf16 = jnp.float32, jnp.bfloat16

    def chunk_bufs(*lead):
        return [pltpu.VMEM((*lead, cls_dev, chunk_lanes(g)), f32) for g in range(CHUNKS)]

    dma = pltpu.SemaphoreType.DMA
    out = pl.pallas_call(
        functools.partial(kernel, ni, no, cls_dev),
        out_shape=jax.ShapeDtypeStruct((cls_dev, FLAT + rows), f32),
        in_specs=[vmem] * 5,
        out_specs=vmem,
        scratch_shapes=[
            pltpu.VMEM((LANES, LANES), f32),
            pltpu.VMEM((LANES, LANES), f32),
            pltpu.VMEM((cls_count * WIRE, LANES), f32),
            pltpu.VMEM((ni, no, cls_dev * WIRE, LANES), bf16),
            pltpu.VMEM((TURNS * cls_count, FLAT), bf16),
            pltpu.VMEM((2, 8, rows), jnp.int32),
            pltpu.VMEM((2, 8, rows), f32),
            pltpu.VMEM((FLAT, rows), f32),
            pltpu.VMEM((ANGLES, 8, rows), f32),
            pltpu.VMEM((FLAT, rows), f32),
            pltpu.VMEM(((ANGLES + EXT) * RADII, 2 * rows), bf16),
            *chunk_bufs(ni, no), *chunk_bufs(ni, no), *chunk_bufs(no), *chunk_bufs(no),
            dma((no,)), dma((no,)), dma((ni,)), dma((ni,)), dma((ni,)), dma((ni,)),
            dma((CHUNKS, ni)), dma((CHUNKS, ni)), dma((CHUNKS, no)), dma((CHUNKS, no)),
            dma((2,)), dma((2,)),
        ],
        compiler_params=pltpu.CompilerParams(
            collective_id=0, has_side_effects=True, vmem_limit_bytes=56 * 1024 * 1024),
    )(particles, references, classes.reshape(1, half), angles.reshape(1, half), weights.reshape(1, half))
    return out[0, FLAT:FLAT + half], out[:, :FLAT]


def solution(mesh):
    return jax.shard_map(
        local,
        mesh=mesh,
        in_specs=(
            P("loop", None),
            P(("loop", "grp"), None),
            P(("loop", "grp")),
            P(("loop", "grp")),
            P(("loop", "grp")),
        ),
        out_specs=(P(("loop", "grp")), P(("loop", "grp"), None)),
        check_vma=False,
    )
```

time: 28.6 us -> 26.7 us (0.934)
  the two profiles are of different devices: /device:TPU:15 before, /device:TPU:0 now
where the time goes in v2:
time: 26.7 us; the launch traced here: 26.5 us
  Pallas kernels  23.3 us (87%)
  local copies, waits for them, and re-layouts  2.55 us (10%)
  between operations  0.64 us (2%)
    pallas_call x1, Pallas kernels, local(): pl.pallas_call(functools.partial(kernel, ni, no, cls_dev), out_shape=jax....  23.3 us
    slice x1, local copies, waits for them, and re-layouts, local(): return (out[0, FLAT:FLAT + half], out[:, :FLAT])  1.36 us
    squeeze x1, local copies, waits for them, and re-layouts, local(): return (out[0, FLAT:FLAT + half], out[:, :FLAT])  1.2 us

profile of v2, /device:TPU:0, one launch (start us, length us, event | category | flops | bytes accessed | tf_op | source)
XLA Modules:
  0.0 26.5 jit_solution(13658735347970235955)
XLA Ops:
  0.6 23.3 %shard_map.68 = f32[2,3584]{1,0:T(2,128)} custom-call(bf16[128,3456]{1,0:T(8,128)(2,1)} %x_ref.1, bf16[2,3456]{1,0:T(2,128)(2,1)} %ref_ref.1, s32[1,64]{1,0:T(1,128)} %bitcast.5, s32[1,64]{1,0:T(1,128)} %bitcast.6, s32[1,64]{1,0:T(1,128)} %bitcast.7), custom_call_target="tpu_custom_call" | custom-call | tf_op jit(solution)/shard_map/pallas_call | solution.py:269
  23.9 1.2 %slice_bitcast_fusion = f32[64]{0:T(128)} fusion(f32[2,3584]{1,0:T(2,128)} %shard_map.68), kind=kLoop, calls=%fused_computation | loop fusion | bytes 512 | tf_op jit(solution)/shard_map/squeeze | solution.py:294
  25.1 1.4 %slice.7 = f32[2,3456]{1,0:T(2,128)} slice(f32[2,3584]{1,0:T(2,128)} %shard_map.68), slice={[0:2], [0:3456]} | slice | bytes 55296 | tf_op jit(solution)/shard_map/slice | solution.py:294

commit v3 on v2

--- a/solution.py
+++ b/solution.py
@@ -16,11 +16,11 @@
 WIRE = 32
 STEP = 8
 TURNS = ANGLES // STEP
+ODD = ANGLES + 1
 EXT = STEP - 2
 CHUNKS = 3
 CHUNK_R = RADII // CHUNKS
 CHUNK = FLAT // CHUNKS
-WINDOW = 24
 INNER = 4
 SCALE = 2.0 / math.sqrt(FLAT)
 MESH = pl.DeviceIdType.MESH
@@ -34,7 +34,7 @@
     ni, no, cls_dev,
     x_ref, ref_ref, cls_ref, ang_ref, wgt_ref,
     out_ref,
-    square, turned, wide, wire, rbig, lab, stat, flat_t, ping, flat_a, ptx,
+    square, turned, wide, wire, rbig, lab, stat, flat_t, padded, flat_a, ptx,
     part0, part1, part2, gota0, gota1, gota2, sum0, sum1, sum2, gotb0, gotb1, gotb2,
     z_send, z_recv, i_send, i_recv, f_send, f_recv, a_send, a_recv, b_send, b_recv, c_send, c_recv,
 ):
@@ -140,25 +140,22 @@
     named = (((owner % no) * ni + owner // no) * 2 + grp) * cls_dev + row % cls_dev
     pick = jnp.where(named == classes, weights, 0).astype(jnp.float32).astype(jnp.bfloat16)
 
+    sub = lax.broadcasted_iota(jnp.int32, (8, rows), 0)
+
     def chunk_sums(g):
-        for r in range(g * CHUNK_R, (g + 1) * CHUNK_R, 8):
+        for r in range(g * CHUNK_R, (g + 1) * CHUNK_R):
             base = r * ANGLES
-            for t0 in range(0, ANGLES, WINDOW):
-                vals = {t: flat_t[pl.ds(base + t % ANGLES, 8, stride=ANGLES), :]
-                        for t in range(t0 - 7, t0 + WINDOW)}
-                for b in range(3):
-                    low = t0 - 7 + (2 << b) - 1
-                    vals = {t: jnp.where(bits[b], vals[t - (1 << b)], vals[t])
-                            for t in range(low, t0 + WINDOW)}
-                for t in range(t0, t0 + WINDOW):
-                    ping[t] = vals[t]
-            for v in range(STEP):
-                vals = [ping[STEP * u + v] for u in range(TURNS)]
-                for b in range(4):
-                    vals = [jnp.where(bits[3 + b], vals[(u - (1 << b)) % TURNS], vals[u])
-                            for u in range(TURNS)]
-                for u in range(TURNS):
-                    flat_a[pl.ds(base + STEP * u + v, 8, stride=ANGLES), :] = vals[u]
+            vals = [flat_t[base + STEP * u:base + STEP * (u + 1), :] for u in range(TURNS)]
+            for b in range(4):
+                vals = [jnp.where(bits[3 + b], vals[(u - (1 << b)) % TURNS], vals[u])
+                        for u in range(TURNS)]
+            for b in range(3):
+                by = 1 << b
+                moved = [pltpu.roll(v, by, 0) for v in vals]
+                vals = [jnp.where(bits[b], jnp.where(sub < by, moved[(u - 1) % TURNS], moved[u]), vals[u])
+                        for u in range(TURNS)]
+            for u in range(TURNS):
+                flat_a[base + STEP * u:base + STEP * (u + 1), :] = vals[u]
         aligned = flat_a[g * CHUNK:(g + 1) * CHUNK, :].astype(jnp.bfloat16)
         if g == 0:
             aligned = jnp.concatenate([aligned, jnp.ones((LANES, rows), jnp.bfloat16)], axis=0)
@@ -181,8 +178,10 @@
     for g in range(1, CHUNKS):
         chunk_sums(g)
 
+    for r in range(RADII):
+        padded[r * ODD:r * ODD + ANGLES, :] = flat_t[r * ANGLES:(r + 1) * ANGLES, :]
     for t in range(ANGLES):
-        low = flat_t[pl.ds(t, RADII, stride=ANGLES), :].astype(jnp.bfloat16)
+        low = padded[pl.ds(t, RADII, stride=ODD), :].astype(jnp.bfloat16)
         for shift in range(2):
             for at in (t + shift + EXT, t + shift + EXT - ANGLES):
                 if 0 <= at < ANGLES + EXT:
@@ -206,9 +205,13 @@
         i_copy(k).wait()
         f_copy(k).wait()
 
-    wide[...] = wire[...].reshape(cls_count * WIRE, LANES).astype(jnp.float32)
+    for k in range(ni * no):
+        for c in range(cls_dev):
+            block = wire[k // no, k % no, c * WIRE:(c + 1) * WIRE, :].astype(jnp.float32)
+            at = (k * cls_dev + c) * (WIRE + 1)
+            wide[at:at + WIRE, :] = block
     for i in range(TILES):
-        tile = wide[pl.ds(i, cls_count, stride=WIRE), :].astype(jnp.bfloat16)
+        tile = wide[pl.ds(i, cls_count, stride=WIRE + 1), :].astype(jnp.bfloat16)
         for s1 in range(TURNS):
             at = (i - 3 * s1) % TILES
             rbig[s1 * cls_count:(s1 + 1) * cls_count, at * LANES:(at + 1) * LANES] = tile
@@ -230,7 +233,6 @@
     stat_copy = core_copy(stat, 1)
     stat_copy.start()
 
-    weight = None
     for g in range(CHUNKS):
         @pl.loop(1, no)
         def _(k):
@@ -239,16 +241,21 @@
         acc = sums[g][outer]
         for k in range(1, no):
             acc = acc + gotb[g][k]
-        if weight is None:
-            weight = acc[:, CHUNK:CHUNK + 1]
-        out_ref[:, g * CHUNK:(g + 1) * CHUNK] = acc[:, :CHUNK] / weight
+        out_ref[:, g * CHUNK:(g + 1) * CHUNK] = acc[:, :CHUNK]
+        if g == 0:
+            out_ref[:, FLAT:FLAT + LANES] = acc[:, CHUNK:]
 
     stat_copy.wait()
     top2, total2 = stat[1, 0:1, :], stat[1, 1:2, :]
     high = jnp.maximum(top, top2)
     out = high + jnp.log(total * jnp.exp(top - high) + total2 * jnp.exp(top2 - high))
     out = jnp.where(grp == 0, out, jnp.concatenate([out[:, half:], out[:, :half]], axis=1))
-    out_ref[:, FLAT:] = jnp.broadcast_to(out, (cls_dev, rows))
+    out_ref[:, FLAT + LANES:] = jnp.broadcast_to(out, (cls_dev, rows))
+
+
+def finish(sums_ref, logev_ref, avg_ref):
+    avg_ref[...] = sums_ref[:, :FLAT] / sums_ref[:, FLAT:FLAT + 1]
+    logev_ref[...] = sums_ref[0:1, FLAT + LANES:FLAT + LANES + logev_ref.shape[1]]
 
 
 def local(particles, references, classes, angles, weights):
@@ -268,19 +275,19 @@
     dma = pltpu.SemaphoreType.DMA
     out = pl.pallas_call(
         functools.partial(kernel, ni, no, cls_dev),
-        out_shape=jax.ShapeDtypeStruct((cls_dev, FLAT + rows), f32),
+        out_shape=jax.ShapeDtypeStruct((cls_dev, FLAT + LANES + rows), f32),
         in_specs=[vmem] * 5,
         out_specs=vmem,
         scratch_shapes=[
             pltpu.VMEM((LANES, LANES), f32),
             pltpu.VMEM((LANES, LANES), f32),
-            pltpu.VMEM((cls_count * WIRE, LANES), f32),
+            pltpu.VMEM((cls_count * (WIRE + 1), LANES), f32),
             pltpu.VMEM((ni, no, cls_dev * WIRE, LANES), bf16),
             pltpu.VMEM((TURNS * cls_count, FLAT), bf16),
             pltpu.VMEM((2, 8, rows), jnp.int32),
             pltpu.VMEM((2, 8, rows), f32),
             pltpu.VMEM((FLAT, rows), f32),
-            pltpu.VMEM((ANGLES, 8, rows), f32),
+            pltpu.VMEM((RADII * ODD, rows), f32),
             pltpu.VMEM((FLAT, rows), f32),
             pltpu.VMEM(((ANGLES + EXT) * RADII, 2 * rows), bf16),
             *chunk_bufs(ni, no), *chunk_bufs(ni, no), *chunk_bufs(no), *chunk_bufs(no),
@@ -289,9 +296,18 @@
             dma((2,)), dma((2,)),
         ],
         compiler_params=pltpu.CompilerParams(
-            collective_id=0, has_side_effects=True, vmem_limit_bytes=56 * 1024 * 1024),
+            collective_id=0, has_side_effects=True, vmem_limit_bytes=(16 + n // 2) * 1024 * 1024),
     )(particles, references, classes.reshape(1, half), angles.reshape(1, half), weights.reshape(1, half))
-    return out[0, FLAT:FLAT + half], out[:, :FLAT]
+    logev, avg = pl.pallas_call(
+        finish,
+        out_shape=(
+            jax.ShapeDtypeStruct((1, half), f32),
+            jax.ShapeDtypeStruct((cls_dev, FLAT), f32),
+        ),
+        in_specs=[vmem],
+        out_specs=(vmem, vmem),
+    )(out)
+    return logev.reshape(half), avg
 
 
 def solution(mesh):

time: 26.7 us -> 26.9 us (level)
  local copies, waits for them, and re-layouts: 2.55 us -> 3.14 us
  Pallas kernels: 23.3 us -> 22.8 us
    unnamed x0 -> x12, local copies, waits for them, and re-layouts: none -> 3.14 us
    pallas_call x1, Pallas kernels: 23.3 us -> 21.3 us  [local(): pl.pallas_call(functools.partial(kernel, ni, no, cls_dev), out_shape=jax....]
    pallas_call x0 -> x1, Pallas kernels: none -> 1.44 us  [local(): pl.pallas_call(finish, out_shape=(jax.ShapeDtypeStruct((1, half), f32), j...]
    slice x1 -> x0, local copies, waits for them, and re-layouts: 1.36 us -> none  [local(): return (out[0, FLAT:FLAT + half], out[:, :FLAT])]
    squeeze x1 -> x0, local copies, waits for them, and re-layouts: 1.2 us -> none  [local(): return (out[0, FLAT:FLAT + half], out[:, :FLAT])]
where the time goes in v3:
time: 26.9 us; the launch traced here: 26.6 us
  Pallas kernels  22.8 us (85%)
  local copies, waits for them, and re-layouts  3.14 us (12%)
  between operations  0.67 us (2%)
    pallas_call x1, Pallas kernels, local(): pl.pallas_call(functools.partial(kernel, ni, no, cls_dev), out_shape=jax....  21.3 us
    unnamed x12, local copies, waits for them, and re-layouts  3.14 us
    pallas_call x1, Pallas kernels, local(): pl.pallas_call(finish, out_shape=(jax.ShapeDtypeStruct((1, half), f32), j...  1.44 us

profile of v3, /device:TPU:0, one launch (start us, length us, event | category | flops | bytes accessed | tf_op | source)
XLA Modules:
  0.0 26.6 jit_solution(11275181101119235547)
XLA Ops:
  0.6 0.0 copy-start.3
  0.6 0.0 copy-start.4
  0.7 0.0 copy-start.5
  0.7 0.6 %copy-done.3 = s32[64]{0:T(128)S(1)} copy-done((s32[64]{0:T(128)S(1)}, s32[64]{0:T(128)}, u32[]{:S(2)}) %copy-start.3) | copy-done | bytes 280
  1.3 0.0 copy-done.4
  1.3 0.0 copy-done.5
  1.3 0.0 copy-start
  1.3 1.2 %copy-done = bf16[128,3456]{1,0:T(8,128)(2,1)S(1)} copy-done((bf16[128,3456]{1,0:T(8,128)(2,1)S(1)}, bf16[128,3456]{1,0:T(8,128)(2,1)}, u32[]{:S(2)}) %copy-start) | copy-done | bytes 884760
  2.5 0.0 copy-start.2
  2.5 0.7 %copy-done.2 = bf16[2,3456]{1,0:T(2,128)(2,1)S(1)} copy-done((bf16[2,3456]{1,0:T(2,128)(2,1)S(1)}, bf16[2,3456]{1,0:T(2,128)(2,1)}, u32[]{:S(2)}) %copy-start.2) | copy-done | bytes 13848
  3.2 21.3 %shard_map.68.sums_ref = f32[2,3712]{1,0:T(2,128)S(1)} custom-call(bf16[128,3456]{1,0:T(8,128)(2,1)S(1)} %copy-done, bf16[2,3456]{1,0:T(2,128)(2,1)S(1)} %copy-done.2, s32[1,64]{1,0:T(1,128)S(1)} %bitcast.4, s32[1,64]{1,0:T(1,128)S(1)} %bitcast.5, s32[1,64]{1,0:T(1,128)S(1)} %bitcast.6), custom_call_target="tpu_custom_call" | custom-call | tf_op jit(solution)/shard_map/pallas_call | solution.py:276
  24.5 0.0 copy-start.1
  24.5 0.6 %copy-done.1 = f32[2,3712]{1,0:T(2,128)} copy-done((f32[2,3712]{1,0:T(2,128)}, f32[2,3712]{1,0:T(2,128)S(1)}, u32[]{:S(2)}) %copy-start.1) | copy-done | bytes 29720
  25.1 1.4 %shard_map.69 = (f32[1,64]{1,0:T(1,128)}, f32[2,3456]{1,0:T(2,128)}) custom-call(f32[2,3712]{1,0:T(2,128)} %copy-done.1), custom_call_target="tpu_custom_call" | custom-call | tf_op jit(solution)/shard_map/pallas_call | solution.py:301
Async XLA Ops:
  0.6 0.7 %copy-start.3 = (s32[64]{0:T(128)S(1)}, s32[64]{0:T(128)}, u32[]{:S(2)}) copy-start(s32[64]{0:T(128)} %param.7) | copy-start | bytes 772
  0.6 0.7 %copy-start.4 = (s32[64]{0:T(128)S(1)}, s32[64]{0:T(128)}, u32[]{:S(2)}) copy-start(s32[64]{0:T(128)} %param.8) | copy-start | bytes 772
  0.7 0.7 %copy-start.5 = (s32[64]{0:T(128)S(1)}, s32[64]{0:T(128)}, u32[]{:S(2)}) copy-start(s32[64]{0:T(128)} %param.9) | copy-start | bytes 772
  1.3 1.2 %copy-start = (bf16[128,3456]{1,0:T(8,128)(2,1)S(1)}, bf16[128,3456]{1,0:T(8,128)(2,1)}, u32[]{:S(2)}) copy-start(bf16[128,3456]{1,0:T(8,128)(2,1)} %x_ref.1) | copy-start | bytes 2654212
  2.5 0.7 %copy-start.2 = (bf16[2,3456]{1,0:T(2,128)(2,1)S(1)}, bf16[2,3456]{1,0:T(2,128)(2,1)}, u32[]{:S(2)}) copy-start(bf16[2,3456]{1,0:T(2,128)(2,1)} %ref_ref.1) | copy-start | bytes 41476
  24.5 0.6 %copy-start.1 = (f32[2,3712]{1,0:T(2,128)}, f32[2,3712]{1,0:T(2,128)S(1)}, u32[]{:S(2)}) copy-start(f32[2,3712]{1,0:T(2,128)S(1)} %shard_map.68.sums_ref) | copy-start | bytes 89092

commit v4 on v3

--- a/solution.py
+++ b/solution.py
@@ -32,8 +32,9 @@
 
 def kernel(
     ni, no, cls_dev,
-    x_ref, ref_ref, cls_ref, ang_ref, wgt_ref,
+    x_hbm, ref_hbm, cls_hbm, ang_hbm, wgt_hbm,
     out_ref,
+    x_ref, ref_ref, cls_ref, ang_ref, wgt_ref, x_sem, in_sem,
     square, turned, wide, wire, rbig, lab, stat, flat_t, padded, flat_a, ptx,
     part0, part1, part2, gota0, gota1, gota2, sum0, sum1, sum2, gotb0, gotb1, gotb2,
     z_send, z_recv, i_send, i_recv, f_send, f_recv, a_send, a_recv, b_send, b_recv, c_send, c_recv,
@@ -89,13 +90,17 @@
         pl.semaphore_signal(barrier, inc=1, device_id=inner_peer(k), device_id_type=MESH)
     pl.semaphore_signal(barrier, inc=1, device_id=other, device_id_type=MESH)
 
-    lane = lax.broadcasted_iota(jnp.int32, (1, rows), 1)
-    mine = (lane // half) == grp
-    lab[0] = jnp.zeros((8, rows), jnp.int32)
-    for i, src in enumerate((cls_ref, ang_ref, wgt_ref)):
-        both = jnp.concatenate([src[...], src[...]], axis=1)
-        lab[0, i:i + 1, :] = jnp.where(mine, both, 0)
-
+    small = [pltpu.make_async_copy(src, dst, in_sem.at[i]) for i, (src, dst) in enumerate((
+        (ref_hbm, ref_ref), (cls_hbm, cls_ref), (ang_hbm, ang_ref), (wgt_hbm, wgt_ref)))]
+    for copy in small:
+        copy.start()
+    big = []
+    for g in range(CHUNKS):
+        sl = slice(g * CHUNK, (g + 1) * CHUNK)
+        big.append(pltpu.make_async_copy(x_hbm.at[:, sl], x_ref.at[:, sl], x_sem.at[g]))
+        big[-1].start()
+
+    small[0].wait()
     refs = ref_ref[...].astype(jnp.float32)
     square[...] = jnp.zeros((LANES, LANES), jnp.float32)
     wide[0:cls_dev * WIRE, :] = jnp.zeros((cls_dev * WIRE, LANES), jnp.float32)
@@ -109,10 +114,20 @@
             wide[pl.ds(c * WIRE + w, TURNS, stride=3), :] = line[:, w * LANES:(w + 1) * LANES]
     wire[0, 0] = wide[0:cls_dev * WIRE, :].astype(jnp.bfloat16)
 
+    for copy in small[1:]:
+        copy.wait()
+    lane = lax.broadcasted_iota(jnp.int32, (1, rows), 1)
+    mine = (lane // half) == grp
+    lab[0] = jnp.zeros((8, rows), jnp.int32)
+    for i, src in enumerate((cls_ref, ang_ref, wgt_ref)):
+        both = jnp.concatenate([src[...], src[...]], axis=1)
+        lab[0, i:i + 1, :] = jnp.where(mine, both, 0)
+
     def transpose(g):
+        big[g].wait()
         for i in range(g * (CHUNK // LANES), (g + 1) * (CHUNK // LANES)):
-            tile = x_ref[:, i * LANES:(i + 1) * LANES].astype(jnp.float32)
-            flat_t[i * LANES:(i + 1) * LANES, :] = tile.T
+            tile = x_ref[:, i * LANES:(i + 1) * LANES].T
+            flat_t[i * LANES:(i + 1) * LANES, :] = tile.astype(jnp.float32)
 
     transpose(0)
     pl.semaphore_wait(barrier, ni + no - 1)
@@ -276,9 +291,16 @@
     out = pl.pallas_call(
         functools.partial(kernel, ni, no, cls_dev),
         out_shape=jax.ShapeDtypeStruct((cls_dev, FLAT + LANES + rows), f32),
-        in_specs=[vmem] * 5,
+        in_specs=[pl.BlockSpec(memory_space=pltpu.HBM)] * 5,
         out_specs=vmem,
         scratch_shapes=[
+            pltpu.VMEM((rows, FLAT), bf16),
+            pltpu.VMEM((cls_dev, FLAT), bf16),
+            pltpu.VMEM((1, half), jnp.int32),
+            pltpu.VMEM((1, half), jnp.int32),
+            pltpu.VMEM((1, half), jnp.int32),
+            dma((CHUNKS,)),
+            dma((4,)),
             pltpu.VMEM((LANES, LANES), f32),
             pltpu.VMEM((LANES, LANES), f32),
             pltpu.VMEM((cls_count * (WIRE + 1), LANES), f32),
@@ -296,7 +318,7 @@
             dma((2,)), dma((2,)),
         ],
         compiler_params=pltpu.CompilerParams(
-            collective_id=0, has_side_effects=True, vmem_limit_bytes=(16 + n // 2) * 1024 * 1024),
+            collective_id=0, has_side_effects=True, vmem_limit_bytes=56 * 1024 * 1024),
     )(particles, references, classes.reshape(1, half), angles.reshape(1, half), weights.reshape(1, half))
     logev, avg = pl.pallas_call(
         finish,
@@ -306,6 +328,7 @@
         ),
         in_specs=[vmem],
         out_specs=(vmem, vmem),
+        compiler_params=pltpu.CompilerParams(vmem_limit_bytes=2 * 1024 * 1024),
     )(out)
     return logev.reshape(half), avg
 

time: 26.9 us -> 24.4 us (0.907)
  local copies, waits for them, and re-layouts: 3.14 us -> 0.74 us
    unnamed x12 -> x2, local copies, waits for them, and re-layouts: 3.14 us -> 0.74 us
    pallas_call x1, Pallas kernels: 21.3 us -> 22.1 us  [local(): pl.pallas_call(functools.partial(kernel, ni, no, cls_dev), out_shape=jax....]
    pallas_call x1, Pallas kernels: 1.44 us -> 0.69 us  [local(): pl.pallas_call(finish, out_shape=(jax.ShapeDtypeStruct((1, half), f32), j...]
where the time goes in v4:
time: 24.4 us; the launch traced here: 24.2 us
  Pallas kernels  22.8 us (93%)
  local copies, waits for them, and re-layouts  0.74 us (3%)
  between operations  0.65 us (3%)
    pallas_call x1, Pallas kernels, local(): pl.pallas_call(functools.partial(kernel, ni, no, cls_dev), out_shape=jax....  22.1 us
    unnamed x2, local copies, waits for them, and re-layouts  0.74 us
    pallas_call x1, Pallas kernels, local(): pl.pallas_call(finish, out_shape=(jax.ShapeDtypeStruct((1, half), f32), j...  0.69 us

profile of v4, /device:TPU:0, one launch (start us, length us, event | category | flops | bytes accessed | tf_op | source)
XLA Modules:
  0.0 24.2 jit_solution(17195545286091493995)
XLA Ops:
  0.6 22.1 %shard_map.68.sums_ref = f32[2,3712]{1,0:T(2,128)} custom-call(bf16[128,3456]{1,0:T(8,128)(2,1)} %x_hbm.1, bf16[2,3456]{1,0:T(2,128)(2,1)} %ref_hbm.1, s32[1,64]{1,0:T(1,128)} %bitcast.4, s32[1,64]{1,0:T(1,128)} %bitcast.5, s32[1,64]{1,0:T(1,128)} %bitcast.6), custom_call_target="tpu_custom_call" | custom-call | tf_op jit(solution)/shard_map/pallas_call | solution.py:291
  22.8 0.0 copy-start
  22.8 0.7 %copy-done = f32[2,3712]{1,0:T(2,128)S(1)} copy-done((f32[2,3712]{1,0:T(2,128)S(1)}, f32[2,3712]{1,0:T(2,128)}, u32[]{:S(2)}) %copy-start) | copy-done | bytes 29720
  23.5 0.7 %shard_map.69 = (f32[1,64]{1,0:T(1,128)}, f32[2,3456]{1,0:T(2,128)}) custom-call(f32[2,3712]{1,0:T(2,128)S(1)} %copy-done), custom_call_target="tpu_custom_call" | custom-call | tf_op jit(solution)/shard_map/pallas_call | solution.py:323
Async XLA Ops:
  22.8 0.8 %copy-start = (f32[2,3712]{1,0:T(2,128)S(1)}, f32[2,3712]{1,0:T(2,128)}, u32[]{:S(2)}) copy-start(f32[2,3712]{1,0:T(2,128)} %shard_map.68.sums_ref) | copy-start | bytes 89092

commit v5 on v4

--- a/solution.py
+++ b/solution.py
@@ -82,8 +82,7 @@
 
     barrier = pltpu.get_barrier_semaphore()
 
-    @pl.loop(1, no)
-    def _(k):
+    for k in range(1, no):
         pl.semaphore_signal(barrier, inc=1, device_id=outer_peer(k), device_id_type=MESH)
 
     for k in range(1, ni):
@@ -135,8 +134,7 @@
     label_copy = core_copy(lab, 0)
     label_copy.start()
 
-    @pl.loop(1, no)
-    def _(k):
+    for k in range(1, no):
         z_copy(k).start()
 
     for k in range(1, ni):
@@ -176,15 +174,15 @@
             aligned = jnp.concatenate([aligned, jnp.ones((LANES, rows), jnp.bfloat16)], axis=0)
         mine_sums = lax.dot_general(pick, aligned, (((1,), (1,)), ((), ())),
                                     preferred_element_type=jnp.float32)
-        for o in range(ni * no):
-            part[g][o // no, o % no] = mine_sums[o * cls_dev:(o + 1) * cls_dev, :]
+        per = no * cls_dev
+        for i in range(ni):
+            part[g][i] = mine_sums[i * per:(i + 1) * per, :]
         for k in range(1, ni):
             a_copy(g, k).start()
 
     chunk_sums(0)
 
-    @pl.loop(1, no)
-    def _(k):
+    for k in range(1, no):
         z_copy(k).wait()
 
     for k in range(1, ni):
@@ -208,10 +206,9 @@
         acc = part[g][inner]
         for k in range(1, ni):
             acc = acc + gota[g][k]
-        sums[g][...] = acc
-
-        @pl.loop(1, no)
-        def _(k):
+        for z in range(no):
+            sums[g][z] = acc[z * cls_dev:(z + 1) * cls_dev, :]
+        for k in range(1, no):
             b_copy(g, k).start()
 
     second(0)
@@ -240,8 +237,9 @@
         for h in range(2):
             tops.append(top[:, h * rows:(h + 1) * rows])
             mass.append(total[:, h * rows:(h + 1) * rows])
-        if q + 1 < CHUNKS:
-            second(q + 1)
+        if q == 1:
+            for g in range(1, CHUNKS):
+                second(g)
     top = functools.reduce(jnp.maximum, tops)
     total = functools.reduce(jnp.add, [m * jnp.exp(t - top) for t, m in zip(tops, mass)])
     stat[0] = jnp.concatenate([top, total, jnp.zeros((6, rows), jnp.float32)], axis=0)
@@ -249,8 +247,7 @@
     stat_copy.start()
 
     for g in range(CHUNKS):
-        @pl.loop(1, no)
-        def _(k):
+        for k in range(1, no):
             b_copy(g, k).wait()
 
         acc = sums[g][outer]
@@ -285,12 +282,12 @@
     f32, bf16 = jnp.float32, jnp.bfloat16
 
     def chunk_bufs(*lead):
-        return [pltpu.VMEM((*lead, cls_dev, chunk_lanes(g)), f32) for g in range(CHUNKS)]
+        return [pltpu.VMEM((*lead, chunk_lanes(g)), f32) for g in range(CHUNKS)]
 
     dma = pltpu.SemaphoreType.DMA
     out = pl.pallas_call(
         functools.partial(kernel, ni, no, cls_dev),
-        out_shape=jax.ShapeDtypeStruct((cls_dev, FLAT + LANES + rows), f32),
+        out_shape=pltpu.VMEM((cls_dev, FLAT + LANES + rows), f32),
         in_specs=[pl.BlockSpec(memory_space=pltpu.HBM)] * 5,
         out_specs=vmem,
         scratch_shapes=[
@@ -312,7 +309,8 @@
             pltpu.VMEM((RADII * ODD, rows), f32),
             pltpu.VMEM((FLAT, rows), f32),
             pltpu.VMEM(((ANGLES + EXT) * RADII, 2 * rows), bf16),
-            *chunk_bufs(ni, no), *chunk_bufs(ni, no), *chunk_bufs(no), *chunk_bufs(no),
+            *chunk_bufs(ni, no * cls_dev), *chunk_bufs(ni, no * cls_dev),
+            *chunk_bufs(no, cls_dev), *chunk_bufs(no, cls_dev),
             dma((no,)), dma((no,)), dma((ni,)), dma((ni,)), dma((ni,)), dma((ni,)),
             dma((CHUNKS, ni)), dma((CHUNKS, ni)), dma((CHUNKS, no)), dma((CHUNKS, no)),
             dma((2,)), dma((2,)),

time: 24.4 us -> 22.5 us (0.922)
  Pallas kernels: 22.8 us -> 21.6 us
  local copies, waits for them, and re-layouts: 0.74 us -> 0 us
    pallas_call x1, Pallas kernels: 22.1 us -> 20.9 us  [local(): pl.pallas_call(functools.partial(kernel, ni, no, cls_dev), out_shape=pltp...]
    unnamed x2 -> x0, local copies, waits for them, and re-layouts: 0.74 us -> none
where the time goes in v5:
time: 22.5 us; the launch traced here: 22.2 us
  Pallas kernels  21.6 us (96%)
  between operations  0.64 us (3%)
    pallas_call x1, Pallas kernels, local(): pl.pallas_call(functools.partial(kernel, ni, no, cls_dev), out_shape=pltp...  20.9 us
    pallas_call x1, Pallas kernels, local(): pl.pallas_call(finish, out_shape=(jax.ShapeDtypeStruct((1, half), f32), j...  0.69 us

profile of v5, /device:TPU:0, one launch (start us, length us, event | category | flops | bytes accessed | tf_op | source)
XLA Modules:
  0.0 22.2 jit_solution(8728423305494376357)
XLA Ops:
  0.6 20.9 %shard_map.68.sums_ref = f32[2,3712]{1,0:T(2,128)S(1)} custom-call(bf16[128,3456]{1,0:T(8,128)(2,1)} %x_hbm.1, bf16[2,3456]{1,0:T(2,128)(2,1)} %ref_hbm.1, s32[1,64]{1,0:T(1,128)} %bitcast.4, s32[1,64]{1,0:T(1,128)} %bitcast.5, s32[1,64]{1,0:T(1,128)} %bitcast.6), custom_call_target="tpu_custom_call" | custom-call | tf_op jit(solution)/shard_map/pallas_call | solution.py:288
  21.6 0.7 %shard_map.69 = (f32[1,64]{1,0:T(1,128)}, f32[2,3456]{1,0:T(2,128)}) custom-call(f32[2,3712]{1,0:T(2,128)S(1)} %shard_map.68.sums_ref), custom_call_target="tpu_custom_call" | custom-call | tf_op jit(solution)/shard_map/pallas_call | solution.py:321

commit v6 on v5

--- a/solution.py
+++ b/solution.py
@@ -18,16 +18,21 @@
 TURNS = ANGLES // STEP
 ODD = ANGLES + 1
 EXT = STEP - 2
-CHUNKS = 3
-CHUNK_R = RADII // CHUNKS
-CHUNK = FLAT // CHUNKS
+CORES = 2
+FETCHES = 3
+FETCH = FLAT // FETCHES
+CORE_R = RADII // CORES
+CORE_FLAT = CORE_R * ANGLES
+CHUNKS = ((0, 16), (16, 8))
+ONES = LANES // 2
+CORE_LANES = CORE_FLAT + ONES
 INNER = 4
 SCALE = 2.0 / math.sqrt(FLAT)
 MESH = pl.DeviceIdType.MESH
 
 
 def chunk_lanes(g):
-    return CHUNK + (LANES if g == 0 else 0)
+    return CHUNKS[g][1] * ANGLES + (ONES if g + 1 == len(CHUNKS) else 0)
 
 
 def kernel(
@@ -36,11 +41,10 @@
     out_ref,
     x_ref, ref_ref, cls_ref, ang_ref, wgt_ref, x_sem, in_sem,
     square, turned, wide, wire, rbig, lab, stat, flat_t, padded, flat_a, ptx,
-    part0, part1, part2, gota0, gota1, gota2, sum0, sum1, sum2, gotb0, gotb1, gotb2,
+    part0, part1, gota0, gota1, sum0, sum1, gotb0, gotb1, keep, swap,
     z_send, z_recv, i_send, i_recv, f_send, f_recv, a_send, a_recv, b_send, b_recv, c_send, c_recv,
 ):
-    part, gota = (part0, part1, part2), (gota0, gota1, gota2)
-    sums, gotb = (sum0, sum1, sum2), (gotb0, gotb1, gotb2)
+    part, gota, sums, gotb = (part0, part1), (gota0, gota1), (sum0, sum1), (gotb0, gotb1)
     me = lax.axis_index("loop")
     grp = lax.axis_index("grp")
     outer, inner = me // ni, lax.rem(me, ni)
@@ -94,8 +98,8 @@
     for copy in small:
         copy.start()
     big = []
-    for g in range(CHUNKS):
-        sl = slice(g * CHUNK, (g + 1) * CHUNK)
+    for g in range(FETCHES):
+        sl = slice(g * FETCH, (g + 1) * FETCH)
         big.append(pltpu.make_async_copy(x_hbm.at[:, sl], x_ref.at[:, sl], x_sem.at[g]))
         big[-1].start()
 
@@ -124,11 +128,10 @@
 
     def transpose(g):
         big[g].wait()
-        for i in range(g * (CHUNK // LANES), (g + 1) * (CHUNK // LANES)):
+        for i in range(g * (FETCH // LANES), (g + 1) * (FETCH // LANES)):
             tile = x_ref[:, i * LANES:(i + 1) * LANES].T
             flat_t[i * LANES:(i + 1) * LANES, :] = tile.astype(jnp.float32)
 
-    transpose(0)
     pl.semaphore_wait(barrier, ni + no - 1)
 
     label_copy = core_copy(lab, 0)
@@ -140,25 +143,28 @@
     for k in range(1, ni):
         i_copy(k).start()
 
-    transpose(1)
-    transpose(2)
+    for g in range(FETCHES):
+        transpose(g)
 
     label_copy.wait()
     labels = lab[0] + lab[1]
     classes, angles, weights = labels[0:1], labels[1:2], labels[2:3]
     bits = [jnp.broadcast_to(((angles >> b) & 1) == 1, (8, rows)) for b in range(7)]
 
-    row = lax.broadcasted_iota(jnp.int32, (cls_count, rows), 0)
-    owner = row // cls_dev
-    named = (((owner % no) * ni + owner // no) * 2 + grp) * cls_dev + row % cls_dev
+    own_cls = CORES * cls_dev
+    per = no * own_cls
+    row = lax.broadcasted_iota(jnp.int32, (ni * per, rows), 0)
+    owner = row // own_cls
+    named = ((owner % no) * ni + owner // no) * own_cls + row % own_cls
     pick = jnp.where(named == classes, weights, 0).astype(jnp.float32).astype(jnp.bfloat16)
-
     sub = lax.broadcasted_iota(jnp.int32, (8, rows), 0)
 
     def chunk_sums(g):
-        for r in range(g * CHUNK_R, (g + 1) * CHUNK_R):
+        first, count = CHUNKS[g]
+        for r in range(first, first + count):
             base = r * ANGLES
-            vals = [flat_t[base + STEP * u:base + STEP * (u + 1), :] for u in range(TURNS)]
+            vals = [flat_t[pl.ds(pl.multiple_of(grp * CORE_FLAT + base + STEP * u, STEP), STEP), :]
+                    for u in range(TURNS)]
             for b in range(4):
                 vals = [jnp.where(bits[3 + b], vals[(u - (1 << b)) % TURNS], vals[u])
                         for u in range(TURNS)]
@@ -169,12 +175,11 @@
                         for u in range(TURNS)]
             for u in range(TURNS):
                 flat_a[base + STEP * u:base + STEP * (u + 1), :] = vals[u]
-        aligned = flat_a[g * CHUNK:(g + 1) * CHUNK, :].astype(jnp.bfloat16)
-        if g == 0:
-            aligned = jnp.concatenate([aligned, jnp.ones((LANES, rows), jnp.bfloat16)], axis=0)
+        aligned = flat_a[first * ANGLES:(first + count) * ANGLES, :].astype(jnp.bfloat16)
+        if g + 1 == len(CHUNKS):
+            aligned = jnp.concatenate([aligned, jnp.ones((ONES, rows), jnp.bfloat16)], axis=0)
         mine_sums = lax.dot_general(pick, aligned, (((1,), (1,)), ((), ())),
                                     preferred_element_type=jnp.float32)
-        per = no * cls_dev
         for i in range(ni):
             part[g][i] = mine_sums[i * per:(i + 1) * per, :]
         for k in range(1, ni):
@@ -188,7 +193,7 @@
     for k in range(1, ni):
         f_copy(k).start()
 
-    for g in range(1, CHUNKS):
+    for g in range(1, len(CHUNKS)):
         chunk_sums(g)
 
     for r in range(RADII):
@@ -207,7 +212,7 @@
         for k in range(1, ni):
             acc = acc + gota[g][k]
         for z in range(no):
-            sums[g][z] = acc[z * cls_dev:(z + 1) * cls_dev, :]
+            sums[g][z] = acc[z * own_cls:(z + 1) * own_cls, :]
         for k in range(1, no):
             b_copy(g, k).start()
 
@@ -238,7 +243,7 @@
             tops.append(top[:, h * rows:(h + 1) * rows])
             mass.append(total[:, h * rows:(h + 1) * rows])
         if q == 1:
-            for g in range(1, CHUNKS):
+            for g in range(1, len(CHUNKS)):
                 second(g)
     top = functools.reduce(jnp.maximum, tops)
     total = functools.reduce(jnp.add, [m * jnp.exp(t - top) for t, m in zip(tops, mass)])
@@ -246,16 +251,18 @@
     stat_copy = core_copy(stat, 1)
     stat_copy.start()
 
-    for g in range(CHUNKS):
+    for g in range(len(CHUNKS)):
         for k in range(1, no):
             b_copy(g, k).wait()
-
         acc = sums[g][outer]
         for k in range(1, no):
             acc = acc + gotb[g][k]
-        out_ref[:, g * CHUNK:(g + 1) * CHUNK] = acc[:, :CHUNK]
-        if g == 0:
-            out_ref[:, FLAT:FLAT + LANES] = acc[:, CHUNK:]
+        low, high = acc[:cls_dev], acc[cls_dev:]
+        at = CHUNKS[g][0] * ANGLES
+        keep[:, at:at + chunk_lanes(g)] = jnp.where(grp == 0, low, high)
+        swap[0, :, at:at + chunk_lanes(g)] = jnp.where(grp == 0, high, low)
+    swap_copy = core_copy(swap, 2)
+    swap_copy.start()
 
     stat_copy.wait()
     top2, total2 = stat[1, 0:1, :], stat[1, 1:2, :]
@@ -264,9 +271,15 @@
     out = jnp.where(grp == 0, out, jnp.concatenate([out[:, half:], out[:, :half]], axis=1))
     out_ref[:, FLAT + LANES:] = jnp.broadcast_to(out, (cls_dev, rows))
 
+    swap_copy.wait()
+    own, theirs = keep[...], swap[1]
+    out_ref[:, :CORE_FLAT] = jnp.where(grp == 0, own, theirs)[:, :CORE_FLAT]
+    out_ref[:, CORE_FLAT:FLAT] = jnp.where(grp == 0, theirs, own)[:, :CORE_FLAT]
+    out_ref[:, FLAT:FLAT + LANES] = own[:, CORE_LANES - LANES:]
+
 
 def finish(sums_ref, logev_ref, avg_ref):
-    avg_ref[...] = sums_ref[:, :FLAT] / sums_ref[:, FLAT:FLAT + 1]
+    avg_ref[...] = sums_ref[:, :FLAT] / sums_ref[:, FLAT + ONES:FLAT + ONES + 1]
     logev_ref[...] = sums_ref[0:1, FLAT + LANES:FLAT + LANES + logev_ref.shape[1]]
 
 
@@ -278,11 +291,12 @@
     ni = INNER
     no = n // ni
     cls_count = n * cls_dev
+    own_cls = CORES * cls_dev
     vmem = pl.BlockSpec(memory_space=pltpu.VMEM)
     f32, bf16 = jnp.float32, jnp.bfloat16
 
     def chunk_bufs(*lead):
-        return [pltpu.VMEM((*lead, chunk_lanes(g)), f32) for g in range(CHUNKS)]
+        return [pltpu.VMEM((*lead, chunk_lanes(g)), f32) for g in range(len(CHUNKS))]
 
     dma = pltpu.SemaphoreType.DMA
     out = pl.pallas_call(
@@ -296,7 +310,7 @@
             pltpu.VMEM((1, half), jnp.int32),
             pltpu.VMEM((1, half), jnp.int32),
             pltpu.VMEM((1, half), jnp.int32),
-            dma((CHUNKS,)),
+            dma((FETCHES,)),
             dma((4,)),
             pltpu.VMEM((LANES, LANES), f32),
             pltpu.VMEM((LANES, LANES), f32),
@@ -307,13 +321,14 @@
             pltpu.VMEM((2, 8, rows), f32),
             pltpu.VMEM((FLAT, rows), f32),
             pltpu.VMEM((RADII * ODD, rows), f32),
-            pltpu.VMEM((FLAT, rows), f32),
+            pltpu.VMEM((CORE_FLAT, rows), f32),
             pltpu.VMEM(((ANGLES + EXT) * RADII, 2 * rows), bf16),
-            *chunk_bufs(ni, no * cls_dev), *chunk_bufs(ni, no * cls_dev),
-            *chunk_bufs(no, cls_dev), *chunk_bufs(no, cls_dev),
+            *chunk_bufs(ni, no * own_cls), *chunk_bufs(ni, no * own_cls),
+            *chunk_bufs(no, own_cls), *chunk_bufs(no, own_cls),
+            pltpu.VMEM((cls_dev, CORE_LANES), f32), pltpu.VMEM((2, cls_dev, CORE_LANES), f32),
             dma((no,)), dma((no,)), dma((ni,)), dma((ni,)), dma((ni,)), dma((ni,)),
-            dma((CHUNKS, ni)), dma((CHUNKS, ni)), dma((CHUNKS, no)), dma((CHUNKS, no)),
-            dma((2,)), dma((2,)),
+            dma((len(CHUNKS), ni)), dma((len(CHUNKS), ni)), dma((len(CHUNKS), no)), dma((len(CHUNKS), no)),
+            dma((3,)), dma((3,)),
         ],
         compiler_params=pltpu.CompilerParams(
             collective_id=0, has_side_effects=True, vmem_limit_bytes=56 * 1024 * 1024),

time: 22.5 us -> 22.7 us (level)
  Pallas kernels: 21.6 us -> 21.9 us
    pallas_call x1, Pallas kernels: 20.9 us -> 21.2 us  [local(): pl.pallas_call(functools.partial(kernel, ni, no, cls_dev), out_shape=pltp...]
where the time goes in v6:
time: 22.7 us; the launch traced here: 22.5 us
  Pallas kernels  21.9 us (96%)
  between operations  0.64 us (3%)
    pallas_call x1, Pallas kernels, local(): pl.pallas_call(functools.partial(kernel, ni, no, cls_dev), out_shape=pltp...  21.2 us
    pallas_call x1, Pallas kernels, local(): pl.pallas_call(finish, out_shape=(jax.ShapeDtypeStruct((1, half), f32), j...  0.69 us

profile of v6, /device:TPU:0, one launch (start us, length us, event | category | flops | bytes accessed | tf_op | source)
XLA Modules:
  0.0 22.5 jit_solution(9556828420472027749)
XLA Ops:
  0.6 21.2 %shard_map.68.sums_ref = f32[2,3712]{1,0:T(2,128)S(1)} custom-call(bf16[128,3456]{1,0:T(8,128)(2,1)} %x_hbm.1, bf16[2,3456]{1,0:T(2,128)(2,1)} %ref_hbm.1, s32[1,64]{1,0:T(1,128)} %bitcast.4, s32[1,64]{1,0:T(1,128)} %bitcast.5, s32[1,64]{1,0:T(1,128)} %bitcast.6), custom_call_target="tpu_custom_call" | custom-call | tf_op jit(solution)/shard_map/pallas_call | solution.py:302
  21.8 0.7 %shard_map.69 = (f32[1,64]{1,0:T(1,128)}, f32[2,3456]{1,0:T(2,128)}) custom-call(f32[2,3712]{1,0:T(2,128)S(1)} %shard_map.68.sums_ref), custom_call_target="tpu_custom_call" | custom-call | tf_op jit(solution)/shard_map/pallas_call | solution.py:336

commit v7 on v5

--- a/solution.py
+++ b/solution.py
@@ -99,6 +99,20 @@
         big.append(pltpu.make_async_copy(x_hbm.at[:, sl], x_ref.at[:, sl], x_sem.at[g]))
         big[-1].start()
 
+    for copy in small[1:]:
+        copy.wait()
+    lane = lax.broadcasted_iota(jnp.int32, (1, rows), 1)
+    mine = (lane // half) == grp
+    lab[0] = jnp.zeros((8, rows), jnp.int32)
+    for i, src in enumerate((cls_ref, ang_ref, wgt_ref)):
+        both = jnp.concatenate([src[...], src[...]], axis=1)
+        lab[0, i:i + 1, :] = jnp.where(mine, both, 0)
+
+    pl.semaphore_wait(barrier, ni + no - 1)
+
+    label_copy = core_copy(lab, 0)
+    label_copy.start()
+
     small[0].wait()
     refs = ref_ref[...].astype(jnp.float32)
     square[...] = jnp.zeros((LANES, LANES), jnp.float32)
@@ -113,35 +127,19 @@
             wide[pl.ds(c * WIRE + w, TURNS, stride=3), :] = line[:, w * LANES:(w + 1) * LANES]
     wire[0, 0] = wide[0:cls_dev * WIRE, :].astype(jnp.bfloat16)
 
-    for copy in small[1:]:
-        copy.wait()
-    lane = lax.broadcasted_iota(jnp.int32, (1, rows), 1)
-    mine = (lane // half) == grp
-    lab[0] = jnp.zeros((8, rows), jnp.int32)
-    for i, src in enumerate((cls_ref, ang_ref, wgt_ref)):
-        both = jnp.concatenate([src[...], src[...]], axis=1)
-        lab[0, i:i + 1, :] = jnp.where(mine, both, 0)
-
     def transpose(g):
         big[g].wait()
         for i in range(g * (CHUNK // LANES), (g + 1) * (CHUNK // LANES)):
             tile = x_ref[:, i * LANES:(i + 1) * LANES].T
             flat_t[i * LANES:(i + 1) * LANES, :] = tile.astype(jnp.float32)
 
-    transpose(0)
-    pl.semaphore_wait(barrier, ni + no - 1)
-
-    label_copy = core_copy(lab, 0)
-    label_copy.start()
-
     for k in range(1, no):
         z_copy(k).start()
 
     for k in range(1, ni):
         i_copy(k).start()
 
-    transpose(1)
-    transpose(2)
+    transpose(0)
 
     label_copy.wait()
     labels = lab[0] + lab[1]
@@ -189,6 +187,7 @@
         f_copy(k).start()
 
     for g in range(1, CHUNKS):
+        transpose(g)
         chunk_sums(g)
 
     for r in range(RADII):
@@ -237,9 +236,8 @@
         for h in range(2):
             tops.append(top[:, h * rows:(h + 1) * rows])
             mass.append(total[:, h * rows:(h + 1) * rows])
-        if q == 1:
-            for g in range(1, CHUNKS):
-                second(g)
+        if 1 <= q < CHUNKS:
+            second(q)
     top = functools.reduce(jnp.maximum, tops)
     total = functools.reduce(jnp.add, [m * jnp.exp(t - top) for t, m in zip(tops, mass)])
     stat[0] = jnp.concatenate([top, total, jnp.zeros((6, rows), jnp.float32)], axis=0)

time: 22.5 us -> 23.5 us (1.044)
  Pallas kernels: 21.6 us -> 22.7 us
    pallas_call x1, Pallas kernels: 20.9 us -> 22 us  [local(): pl.pallas_call(functools.partial(kernel, ni, no, cls_dev), out_shape=pltp...]
where the time goes in v7:
time: 23.5 us; the launch traced here: 23.4 us
  Pallas kernels  22.7 us (97%)
  between operations  0.64 us (3%)
    pallas_call x1, Pallas kernels, local(): pl.pallas_call(functools.partial(kernel, ni, no, cls_dev), out_shape=pltp...  22 us
    pallas_call x1, Pallas kernels, local(): pl.pallas_call(finish, out_shape=(jax.ShapeDtypeStruct((1, half), f32), j...  0.69 us

profile of v7, /device:TPU:0, one launch (start us, length us, event | category | flops | bytes accessed | tf_op | source)
XLA Modules:
  0.0 23.4 jit_solution(4523317516371924847)
XLA Ops:
  0.6 22.0 %shard_map.68.sums_ref = f32[2,3712]{1,0:T(2,128)S(1)} custom-call(bf16[128,3456]{1,0:T(8,128)(2,1)} %x_hbm.1, bf16[2,3456]{1,0:T(2,128)(2,1)} %ref_hbm.1, s32[1,64]{1,0:T(1,128)} %bitcast.4, s32[1,64]{1,0:T(1,128)} %bitcast.5, s32[1,64]{1,0:T(1,128)} %bitcast.6), custom_call_target="tpu_custom_call" | custom-call | tf_op jit(solution)/shard_map/pallas_call | solution.py:286
  22.7 0.7 %shard_map.69 = (f32[1,64]{1,0:T(1,128)}, f32[2,3456]{1,0:T(2,128)}) custom-call(f32[2,3712]{1,0:T(2,128)S(1)} %shard_map.68.sums_ref), custom_call_target="tpu_custom_call" | custom-call | tf_op jit(solution)/shard_map/pallas_call | solution.py:319

commit v8 on v5

--- a/solution.py
+++ b/solution.py
@@ -144,6 +144,12 @@
     transpose(2)
 
     label_copy.wait()
+    for k in range(1, no):
+        z_copy(k).wait()
+
+    for k in range(1, ni):
+        f_copy(k).start()
+
     labels = lab[0] + lab[1]
     classes, angles, weights = labels[0:1], labels[1:2], labels[2:3]
     bits = [jnp.broadcast_to(((angles >> b) & 1) == 1, (8, rows)) for b in range(7)]
@@ -181,12 +187,6 @@
             a_copy(g, k).start()
 
     chunk_sums(0)
-
-    for k in range(1, no):
-        z_copy(k).wait()
-
-    for k in range(1, ni):
-        f_copy(k).start()
 
     for g in range(1, CHUNKS):
         chunk_sums(g)

time: 22.5 us -> 24 us (1.067)
  Pallas kernels: 21.6 us -> 23.1 us
    pallas_call x1, Pallas kernels: 20.9 us -> 22.4 us  [local(): pl.pallas_call(functools.partial(kernel, ni, no, cls_dev), out_shape=pltp...]
where the time goes in v8:
time: 24 us; the launch traced here: 23.7 us
  Pallas kernels  23.1 us (96%)
  between operations  0.64 us (3%)
    pallas_call x1, Pallas kernels, local(): pl.pallas_call(functools.partial(kernel, ni, no, cls_dev), out_shape=pltp...  22.4 us
    pallas_call x1, Pallas kernels, local(): pl.pallas_call(finish, out_shape=(jax.ShapeDtypeStruct((1, half), f32), j...  0.69 us

profile of v8, /device:TPU:0, one launch (start us, length us, event | category | flops | bytes accessed | tf_op | source)
XLA Modules:
  0.0 23.7 jit_solution(10044987371095750809)
XLA Ops:
  0.6 22.4 %shard_map.68.sums_ref = f32[2,3712]{1,0:T(2,128)S(1)} custom-call(bf16[128,3456]{1,0:T(8,128)(2,1)} %x_hbm.1, bf16[2,3456]{1,0:T(2,128)(2,1)} %ref_hbm.1, s32[1,64]{1,0:T(1,128)} %bitcast.4, s32[1,64]{1,0:T(1,128)} %bitcast.5, s32[1,64]{1,0:T(1,128)} %bitcast.6), custom_call_target="tpu_custom_call" | custom-call | tf_op jit(solution)/shard_map/pallas_call | solution.py:288
  23.0 0.7 %shard_map.69 = (f32[1,64]{1,0:T(1,128)}, f32[2,3456]{1,0:T(2,128)}) custom-call(f32[2,3712]{1,0:T(2,128)S(1)} %shard_map.68.sums_ref), custom_call_target="tpu_custom_call" | custom-call | tf_op jit(solution)/shard_map/pallas_call | solution.py:321
